TPU v7x, 32 devices: a whole 2x2x4 slice. The times are simulated.
32 devices in a mesh: tile: 16 (over z, x, core), mem: 2 (over y).
Axes of the slice: x: 2, y: 2, z: 4, core: 2. Of those that a mesh axis runs over, the one named last changes fastest.
Arguments:
- ens: bfloat16 [16, 2400, 256], P('mem', 'tile'), may hold values from -6 to 6
- direction: float32 [2400, 256], P('tile'), may hold values from -6 to 6
- resid: float32 [2400, 256], P('tile'), may hold values from -6 to 6
- increment: float32 [2400, 256], P('tile'), may hold values from -6 to 6
- clim_var: float32 [2400, 256], P('tile'), may hold values from 0.1 to 1
- corr_table: bfloat16 [9, 256, 256], replicated, may hold values from -0.25 to 0.5
- amp_table: float32 [16], replicated, may hold values from 0.25 to 2
- adjacency: int32 [2400, 9], P('tile'), may hold values from 0 to 149, as said below
- block_index: int32 [2400, 9], P('tile'), may hold values from 0 to 15
Outputs:
- new_increment: float32 [2400, 256], P('tile')
- precond: float32 [2400, 256], P('tile')
Inputs may be any that keep to these rules, and one draw needn't show every extreme that they name: `adjacency`: slot 4 of patch p holds p's own column.
All inputs are finite; a program needn't handle non-finite values.
Results may differ from a plain program's by a relative error of at most 0.00072.
Values may be sent and summed in bfloat16 or wider, within the bound.
No kernel may reach another device: no remote copies, remote signals or barrier semaphores. Data moves between devices by JAX's collectives and lax.ppermute only.
A program may use at most 128 MiB of HBM per device.

v0:
```python
import jax
import jax.numpy as jnp
from jax import lax
from jax.sharding import PartitionSpec as P

SLOTS = 9


def extended(shard, sides, width):
    for axis, dim in sides:
        size, length = (lax.axis_size(axis), shard.shape[dim])
        up = [(i, (i + 1) % size) for i in range(size - 1)]
        down = [(j, i) for i, j in up]
        last = lax.slice_in_dim(shard, length - width, length, axis=dim)
        leading = lax.slice_in_dim(shard, 0, width, axis=dim)
        before = lax.ppermute(last, axis, up)
        after = lax.ppermute(leading, axis, down)
        shard = jnp.concatenate([before, shard, after], axis=dim)
    return shard


def neighbour_term(stripes, columns, weights, corr_table, slot_index):
    source = stripes[:, slot_index // 3]
    picked = jnp.take(source, columns[:, slot_index], axis=1)
    flattened = picked.reshape(-1, picked.shape[-1])
    product = jnp.dot(
        flattened, corr_table[slot_index], preferred_element_type=jnp.float32
    ).reshape(picked.shape)
    return product * weights[:, slot_index][None, :, None]


def on_device(
    ens, direction, resid, increment, clim_var, corr_table, amp_table, adjacency, block_index
):
    local_members, patch_count, vec_width = ens.shape
    groups = lax.axis_size("mem")
    members = local_members * groups
    vectors = jnp.stack([direction, resid])
    scaled = (ens.astype(jnp.float32)[None] * vectors[:, None]).astype(jnp.bfloat16)
    scaled = scaled.reshape(2 * local_members, 1, patch_count, vec_width)
    stripes = extended(scaled, (("tile", 1),), 1)
    classes = (
        block_index[:, :, None] == jnp.arange(amp_table.shape[0], dtype=jnp.int32)[None, None, :]
    ).astype(jnp.float32)
    weights = jnp.sum(classes * amp_table[None, None, :], axis=2)
    summed = stripes[:, 1].astype(jnp.float32)
    for slot_index in range(SLOTS):
        summed = summed + neighbour_term(stripes, adjacency, weights, corr_table, slot_index)
    summed = summed.reshape(2, local_members, patch_count, vec_width)
    partial_value = jnp.sum(ens.astype(jnp.float32)[None] * summed, axis=1) / (members - 1)
    applied = lax.psum(partial_value, "mem") + clim_var[None] * vectors
    numerator, denominator = lax.psum(
        (jnp.sum(resid * applied[1]), jnp.sum(direction * applied[0])), "tile"
    )
    step_size = numerator / denominator
    return (increment + step_size * applied[0], applied[1])


def solution(mesh):
    placed = (
        P("mem", "tile", None),
        P("tile", None),
        P("tile", None),
        P("tile", None),
        P("tile", None),
        P(),
        P(),
        P("tile", None),
        P("tile", None),
    )
    return jax.shard_map(
        on_device,
        mesh=mesh,
        in_specs=placed,
        out_specs=(P("tile", None), P("tile", None)),
        check_vma=False,
    )
```

profile of v0, /device:TPU:0, one launch (start us, length us, event | category | flops | bytes accessed | tf_op | source)
XLA Modules:
  0.0 153.1 jit_solution(12614548343102431489)
XLA Ops:
  7.2 0.0 copy-start.4
  7.2 0.0 copy-start.3
  7.2 0.0 all-reduce.3.cloned.1.call-start
  7.2 1.3 copy.28
  8.6 0.2 multiply_convert_fusion
  8.8 0.8 copy-done
  9.6 1.3 copy.63
  10.8 1.3 collective-permute-start.1
  12.1 4.1 %collective-permute-start = (bf16[16,1,150,256]{3,0,2,1:T(8,128)(2,1)}, bf16[16,1,150,256]{3,0,2,1:T(8,128)(2,1)}, u32[]{:S(2)}, u32[]{:S(2)}) collective-permute-start(bf16[16,1,150,256]{3,0,2,1:T(8,128)(2,1)} %bitcast.92), channel_id=1, source_target_pairs={{0,2},{2,4},{4,6},{6,8},{8,10},{10,12},{12,14},{14,16},{16,18},{18... | collective-permute-start | bytes 3686408 | tf_op jit(solution)/shard_map/ppermute | solution.py:16
  16.5 0.2 copy.33
  16.8 1.9 %gather_fusion.5 = bf16[150,16,256]{2,1,0:T(8,128)(2,1)} fusion(bf16[16,150,256]{2,0,1:T(8,128)(2,1)S(1)} %copy.33, s32[1024]{0:T(1024)S(1)} %pad_clamp_fusion.3), kind=kCustom, calls=%fused_computation.5.clone | custom fusion | bytes 2458200 | tf_op jit(solution)/shard_map/jit(_take)/gather | solution.py:24
  18.7 1.9 %gather_fusion.4 = bf16[150,16,256]{2,1,0:T(8,128)(2,1)} fusion(bf16[16,150,256]{2,0,1:T(8,128)(2,1)S(1)} %copy.33, s32[1024]{0:T(1024)S(1)} %pad_clamp_fusion.4), kind=kCustom, calls=%fused_computation.4.clone | custom fusion | bytes 2458200 | tf_op jit(solution)/shard_map/jit(_take)/gather | solution.py:24
  20.6 0.1 select_reduce_fusion
  20.7 1.5 select_bitcast_fusion.3
  22.3 3.3 %fusion.5 = f32[16,150,256]{2,1,0:T(8,128)} fusion(bf16[16,150,256]{2,0,1:T(8,128)(2,1)S(1)} %select_bitcast_fusion.3, bf16[9,256,256]{2,1,0:T(8,128)(2,1)} %param.16), kind=kOutput, calls=%fused_computation.17 | convolution fusion | flops 314572800 | bytes 3817472 | tf_op jit(solution)/shard_map/dot_general | solution.py:26
  25.6 0.2 select_bitcast_fusion.4
  25.8 3.2 %fusion.7 = f32[16,150,256]{2,1,0:T(8,128)} fusion(bf16[16,150,256]{2,0,1:T(8,128)(2,1)S(1)} %select_bitcast_fusion.4, bf16[9,256,256]{2,1,0:T(8,128)(2,1)} %param.16), kind=kOutput, calls=%fused_computation.19 | convolution fusion | flops 314572800 | bytes 3817472 | tf_op jit(solution)/shard_map/dot_general | solution.py:26
  29.1 1.9 %gather_fusion.3 = bf16[150,16,256]{2,1,0:T(8,128)(2,1)} fusion(bf16[16,150,256]{2,0,1:T(8,128)(2,1)S(1)} %copy.33, s32[1024]{0:T(1024)S(1)} %pad_clamp_fusion.5), kind=kCustom, calls=%fused_computation.3.clone | custom fusion | bytes 2458200 | tf_op jit(solution)/shard_map/jit(_take)/gather | solution.py:24
  31.0 1.5 select_bitcast_fusion.5
  32.5 3.3 %fusion.9 = f32[16,150,256]{2,1,0:T(8,128)} fusion(bf16[16,150,256]{2,0,1:T(8,128)(2,1)S(1)} %select_bitcast_fusion.5, bf16[9,256,256]{2,1,0:T(8,128)(2,1)} %param.16), kind=kOutput, calls=%fused_computation.21 | convolution fusion | flops 314572800 | bytes 3817472 | tf_op jit(solution)/shard_map/dot_general | solution.py:26
  35.8 0.0 collective-permute-done.1
  35.8 2.1 %gather_fusion.7 = bf16[150,16,256]{2,1,0:T(8,128)(2,1)S(1)} fusion(bf16[16,150,256]{2,0,1:T(8,128)(2,1)} %bitcast.36, s32[1024]{0:T(1024)S(1)} %pad_clamp_fusion.1), kind=kCustom, calls=%fused_computation.7.clone | custom fusion | bytes 2458200 | tf_op jit(solution)/shard_map/jit(_take)/gather | solution.py:24
  37.9 0.2 select_bitcast_fusion.1
  38.1 3.2 %fusion.1 = f32[16,150,256]{2,1,0:T(8,128)} fusion(bf16[16,150,256]{2,0,1:T(8,128)(2,1)S(1)} %select_bitcast_fusion.1, bf16[9,256,256]{2,1,0:T(8,128)(2,1)} %param.16), kind=kOutput, calls=%fused_computation.13 | convolution fusion | flops 314572800 | bytes 3817472 | tf_op jit(solution)/shard_map/dot_general | solution.py:26
  41.3 0.0 collective-permute-done
  41.3 2.1 %gather_fusion.2 = bf16[150,16,256]{2,1,0:T(8,128)(2,1)S(1)} fusion(bf16[16,150,256]{2,0,1:T(8,128)(2,1)} %bitcast.5, s32[1024]{0:T(1024)S(1)} %pad_clamp_fusion.6), kind=kCustom, calls=%fused_computation.2.clone | custom fusion | bytes 2458200 | tf_op jit(solution)/shard_map/jit(_take)/gather | solution.py:24
  43.5 0.2 select_bitcast_fusion.6
  43.7 3.2 %fusion.11 = f32[16,150,256]{2,1,0:T(8,128)} fusion(bf16[16,150,256]{2,0,1:T(8,128)(2,1)S(1)} %select_bitcast_fusion.6, bf16[9,256,256]{2,1,0:T(8,128)(2,1)} %param.16), kind=kOutput, calls=%fused_computation.23 | convolution fusion | flops 314572800 | bytes 3817472 | tf_op jit(solution)/shard_map/dot_general | solution.py:26
  46.9 2.1 %gather_fusion.1 = bf16[150,16,256]{2,1,0:T(8,128)(2,1)S(1)} fusion(bf16[16,150,256]{2,0,1:T(8,128)(2,1)} %bitcast.5, s32[1024]{0:T(1024)S(1)} %pad_clamp_fusion.7), kind=kCustom, calls=%fused_computation.1.clone | custom fusion | bytes 2458200 | tf_op jit(solution)/shard_map/jit(_take)/gather | solution.py:24
  49.0 0.2 select_bitcast_fusion.7
  49.2 3.2 %fusion.13 = f32[16,150,256]{2,1,0:T(8,128)} fusion(bf16[16,150,256]{2,0,1:T(8,128)(2,1)S(1)} %select_bitcast_fusion.7, bf16[9,256,256]{2,1,0:T(8,128)(2,1)} %param.16), kind=kOutput, calls=%fused_computation.25 | convolution fusion | flops 314572800 | bytes 3817472 | tf_op jit(solution)/shard_map/dot_general | solution.py:26
  52.5 2.1 %gather_fusion = bf16[150,16,256]{2,1,0:T(8,128)(2,1)S(1)} fusion(bf16[16,150,256]{2,0,1:T(8,128)(2,1)} %bitcast.5, s32[1024]{0:T(1024)S(1)} %pad_clamp_fusion.8), kind=kCustom, calls=%fused_computation.clone | custom fusion | bytes 2458200 | tf_op jit(solution)/shard_map/jit(_take)/gather | solution.py:24
  54.6 0.2 select_bitcast_fusion.8
  54.8 3.2 %fusion.15 = f32[16,150,256]{2,1,0:T(8,128)} fusion(bf16[16,150,256]{2,0,1:T(8,128)(2,1)S(1)} %select_bitcast_fusion.8, bf16[9,256,256]{2,1,0:T(8,128)(2,1)} %param.16), kind=kOutput, calls=%fused_computation.27 | convolution fusion | flops 314572800 | bytes 3817472 | tf_op jit(solution)/shard_map/dot_general | solution.py:26
  58.0 2.1 %gather_fusion.6 = bf16[150,16,256]{2,1,0:T(8,128)(2,1)S(1)} fusion(bf16[16,150,256]{2,0,1:T(8,128)(2,1)} %bitcast.36, s32[1024]{0:T(1024)S(1)} %pad_clamp_fusion.2), kind=kCustom, calls=%fused_computation.6.clone | custom fusion | bytes 2458200 | tf_op jit(solution)/shard_map/jit(_take)/gather | solution.py:24
  60.1 0.2 select_bitcast_fusion.2
  60.4 3.2 %fusion.3 = f32[16,150,256]{2,1,0:T(8,128)} fusion(bf16[16,150,256]{2,0,1:T(8,128)(2,1)S(1)} %select_bitcast_fusion.2, bf16[9,256,256]{2,1,0:T(8,128)(2,1)} %param.16), kind=kOutput, calls=%fused_computation.15 | convolution fusion | flops 314572800 | bytes 3817472 | tf_op jit(solution)/shard_map/dot_general | solution.py:26
  63.6 2.1 %gather_fusion.8 = bf16[150,16,256]{2,1,0:T(8,128)(2,1)S(1)} fusion(bf16[16,150,256]{2,0,1:T(8,128)(2,1)} %bitcast.36, s32[1024]{0:T(1024)S(1)} %pad_clamp_fusion), kind=kCustom, calls=%fused_computation.8.clone | custom fusion | bytes 2458200 | tf_op jit(solution)/shard_map/jit(_take)/gather | solution.py:24
  65.7 0.2 select_bitcast_fusion
  65.9 1.0 copy-done.1
  67.0 8.2 %multiply_reduce_fusion = f32[2,150,256]{2,1,0:T(8,128)S(1)} fusion(f32[8,150,256]{2,1,0:T(8,128)S(1)} %copy-done.1, f32[150]{0:T(256)S(1)} %bitcast.100, bf16[9,256,256]{2,1,0:T(8,128)(2,1)} %param.16, bf16[16,150,256]{2,0,1:T(8,128)(2,1)S(1)} %select_bitcast_fusion, f32[16,150,256]{2,1,0:T(8,128)} %fusion.1, f32[150]{0:T(256)S(1)} %bitcast.101, ...), kind=kOutput, calls=%fused_computation.9 | convolution fusion | flops 327398400 | bytes 24053016 | tf_op jit(solution)/shard_map/dot_general | solution.py:26
  75.2 0.7 broadcast_multiply_fusion
  75.9 0.0 all-reduce.3.cloned.1.call-update
  76.0 32.0 %all-reduce.3.cloned.1.call-done = f32[2,150,256]{2,1,0:T(8,128)} async-done(((f32[2,150,256]{2,1,0:T(8,128)}), f32[2,150,256]{2,1,0:T(8,128)}) %all-reduce.3.cloned.1.call-update) | async-done | bytes 307216 | tf_op jit(solution)/shard_map/psum | solution.py:51
  108.0 1.0 multiply_add_fusion.1
  109.0 1.3 multiply_reduce_fusion.2
  110.3 33.9 %all-reduce = (f32[]{:T(128)}, f32[]{:T(128)}) all-reduce(f32[]{:T(128)} %get-tuple-element.5, f32[]{:T(128)} %get-tuple-element.7), channel_id=1, replica_groups=mesh['tile'=16,'mem'=2] {'tile'}, use_global_device_ids=true, to_apply=%region_4.6 | all-reduce | flops 2 | bytes 16 | tf_op jit(solution)/shard_map/psum | solution.py:52
  145.6 0.7 multiply_add_fusion.2
  (46 shorter events, 0.2 us)
Async XLA Ops:
  7.2 1.4 copy-start.4
  7.2 1.4 copy-start.3
  7.2 100.8 %all-reduce.3.cloned.1.call-start = ((), (), s32[]{:S(2)}) async-start(), calls=%async_computation | async-start | bytes 622592 | tf_op jit(solution)/shard_map/psum | solution.py:51
  8.5 1.1 copy-start
  9.6 6.7 %copy-start.8 = (s32[150,9]{0,1:T(8,128)S(1)}, s32[150,9]{0,1:T(8,128)}, u32[]{:S(2)}) copy-start(s32[150,9]{0,1:T(8,128)} %param.18) | copy-start | bytes 16204
  10.8 24.9 %collective-permute-start.1 = (bf16[16,1,150,256]{3,0,2,1:T(8,128)(2,1)}, bf16[16,1,150,256]{3,0,2,1:T(8,128)(2,1)}, u32[]{:S(2)}, u32[]{:S(2)}) collective-permute-start(bf16[16,1,150,256]{3,0,2,1:T(8,128)(2,1)} %bitcast.92), channel_id=1, source_target_pairs={{2,0},{4,2},{6,4},{8,6},{10,8},{12,10},{14,12},{16,14},{18,16},{20... | collective-permute-start | bytes 3686408 | tf_op jit(solution)/shard_map/ppermute | solution.py:17
  12.1 29.2 %collective-permute-start = (bf16[16,1,150,256]{3,0,2,1:T(8,128)(2,1)}, bf16[16,1,150,256]{3,0,2,1:T(8,128)(2,1)}, u32[]{:S(2)}, u32[]{:S(2)}) collective-permute-start(bf16[16,1,150,256]{3,0,2,1:T(8,128)(2,1)} %bitcast.92), channel_id=1, source_target_pairs={{0,2},{2,4},{4,6},{6,8},{8,10},{10,12},{12,14},{14,16},{16,18},{18... | collective-permute-start | bytes 3686408 | tf_op jit(solution)/shard_map/ppermute | solution.py:16
  18.7 1.9 %copy-start.7 = (s32[150,9]{0,1:T(8,128)S(1)}, s32[150,9]{0,1:T(8,128)}, u32[]{:S(2)}) copy-start(s32[150,9]{0,1:T(8,128)} %param.19) | copy-start | bytes 16204
  18.7 1.9 %copy-start.9 = (f32[16]{0:T(128)S(1)}, f32[16]{0:T(128)}, u32[]{:S(2)}) copy-start(f32[16]{0:T(128)} %param.17) | copy-start | bytes 196
  22.3 3.3 %copy-start.2 = (bf16[150,16,256]{2,1,0:T(8,128)(2,1)S(1)}, bf16[150,16,256]{2,1,0:T(8,128)(2,1)}, u32[]{:S(2)}) copy-start(bf16[150,16,256]{2,1,0:T(8,128)(2,1)} %gather_fusion.4) | copy-start | bytes 3686404
  65.7 1.3 copy-start.1
  67.0 41.0 %copy-start.6 = (f32[150,256]{1,0:T(8,128)S(1)}, f32[150,256]{1,0:T(8,128)}, u32[]{:S(2)}) copy-start(f32[150,256]{1,0:T(8,128)} %param.15) | copy-start | bytes 460804
  75.9 69.6 %copy-start.5 = (f32[150,256]{1,0:T(8,128)S(1)}, f32[150,256]{1,0:T(8,128)}, u32[]{:S(2)}) copy-start(f32[150,256]{1,0:T(8,128)} %param.14) | copy-start | bytes 460804
Sparse Core Ops, SparseCore 0:
  76.1 31.8 all-reduce.2
where the time goes:
time: 154 us; the launch traced here: 153 us
  matrix products  34.1 us (22%)
  blocking collectives  33.9 us (22%)
  waiting for transfers between devices  32 us (21%)
  local copies, waits for them, and re-layouts  22.9 us (15%)
  between operations  15.8 us (10%)
  other arithmetic  8.94 us (6%)
  starting transfers between devices  5.42 us (4%)
    dot_general x9, matrix products, neighbour_term(): jnp.dot(flattened, corr_table[slot_index], preferred_element_type=jnp.flo...  34.1 us
    psum x1, blocking collectives, on_device(): lax.psum((jnp.sum(resid * applied[1]), jnp.sum(direction * applied[0])),...  33.9 us
    psum x1, waiting for transfers between devices, on_device(): applied = lax.psum(partial_value, 'mem') + clim_var[None] * vectors  32 us
    gather x9, local copies, waits for them, and re-layouts, neighbour_term(): picked = jnp.take(source, columns[:, slot_index], axis=1)  18.3 us
    select_n x18, other arithmetic, neighbour_term(): picked = jnp.take(source, columns[:, slot_index], axis=1)  4.65 us
    ppermute x1, starting transfers between devices, extended(): before = lax.ppermute(last, axis, up)  4.11 us
  transfers between devices with their start and end apart: 3, of which 1 were waited for; matrix products, arithmetic and copies ran while one was open for 16% of the time, Pallas kernels for 0%

commit v1 on v0

v1 whole, which is shorter than its diff:
```python
import functools

import jax
import jax.numpy as jnp
from jax import lax
from jax.experimental import pallas as pl
from jax.experimental.pallas import tpu as pltpu
from jax.sharding import PartitionSpec as P

SLOTS = 9
BLOCK = 25
F32 = jnp.float32
BF16 = jnp.bfloat16
VMEM = pl.BlockSpec(memory_space=pltpu.VMEM)
SMEM = pl.BlockSpec(memory_space=pltpu.SMEM)


LANES = 128


def patch_major(ens_ref, flat_ref):
    count, patches, width = ens_ref.shape
    for k in range(count):
        member = ens_ref[k].astype(F32)
        for h in range(width // LANES):
            flat_ref[h, pl.ds(k, patches, stride=count), :] = member[
                :, h * LANES : (h + 1) * LANES
            ]


def members_of(flat_ref, p, count):
    at = pl.ds(pl.multiple_of(p * count, count), count)
    return jnp.concatenate([flat_ref[h, at, :] for h in range(flat_ref.shape[0])], axis=1)


def flat_scratch(rows, width):
    return pltpu.VMEM((width // LANES, rows, LANES), F32)


def scale(flat_ref, first_ref, second_ref, scaled_ref):
    patches, rows, _ = scaled_ref.shape
    count = rows // 2

    def body(p, _):
        members = members_of(flat_ref, p, count)
        a = members * first_ref[pl.ds(p, 1), :]
        b = members * second_ref[pl.ds(p, 1), :]
        scaled_ref[p] = jnp.concatenate([a, b], axis=0).astype(BF16)
        return 0

    lax.fori_loop(0, patches, body, 0, unroll=10)


def gathered(scaled_ref, code_ref, code_rows, corr_ref, corr_rows, amp_ref, start, block):
    rows = scaled_ref.shape[1]
    classes = amp_ref.shape[0]
    totals = None
    for row, slot in zip(code_rows, corr_rows):
        codes = [code_ref[row, start + i] for i in range(block)]
        left = jnp.concatenate([scaled_ref[c // classes] for c in codes], axis=0)
        product = jnp.dot(left, corr_ref[slot], preferred_element_type=F32)
        weighted = [
            product[i * rows : (i + 1) * rows] * amp_ref[lax.rem(c, classes)]
            for i, c in enumerate(codes)
        ]
        totals = weighted if totals is None else [t + w for t, w in zip(totals, weighted)]
    return totals


def contract(flat_ref, p, local, count):
    members = members_of(flat_ref, p, count)
    return (
        jnp.sum(members * local[:count], axis=0, keepdims=True),
        jnp.sum(members * local[count:], axis=0, keepdims=True),
    )


def own_kernel(
    inverse, code_ref, amp_ref, ens_ref, direction_ref, resid_ref, corr_ref,
    part_ref, scaled_ref, flat_ref,
):
    count, patches, _ = ens_ref.shape
    patch_major(ens_ref, flat_ref)
    scale(flat_ref, direction_ref, resid_ref, scaled_ref)

    def body(b, _):
        start = b * BLOCK
        totals = gathered(
            scaled_ref, code_ref, (3, 4, 5), corr_ref, (3, 4, 5), amp_ref, start, BLOCK
        )
        for i in range(BLOCK):
            p = start + i
            local = totals[i] + scaled_ref[p].astype(F32)
            first, second = contract(flat_ref, p, local, count)
            part_ref[0, pl.ds(p, 1), :] = first * inverse
            part_ref[1, pl.ds(p, 1), :] = second * inverse
        return 0

    lax.fori_loop(0, patches // BLOCK, body, 0)


def upper_kernel(code_ref, amp_ref, scaled_ref, corr_ref, out_ref, flat_ref):
    patches, rows, _ = scaled_ref.shape

    def body(b, _):
        start = b * BLOCK
        totals = gathered(
            scaled_ref, code_ref, (0, 1, 2), corr_ref, (6, 7, 8), amp_ref, start, BLOCK
        )
        for i in range(BLOCK):
            at = pl.multiple_of((start + i) * rows, rows)
            for h in range(flat_ref.shape[0]):
                flat_ref[h, pl.ds(at, rows), :] = totals[i][:, h * LANES : (h + 1) * LANES]
        return 0

    lax.fori_loop(0, patches // BLOCK, body, 0)
    for m in range(rows):
        for h in range(flat_ref.shape[0]):
            out_ref[m, :, h * LANES : (h + 1) * LANES] = flat_ref[
                h, pl.ds(m, patches, stride=rows), :
            ]


def return_kernel(inverse, ens_ref, upper_ref, out_ref):
    count = ens_ref.shape[0]
    for v in range(2):
        total = ens_ref[0].astype(F32) * upper_ref[v * count]
        for k in range(1, count):
            total = total + ens_ref[k].astype(F32) * upper_ref[v * count + k]
        out_ref[v] = total * inverse


def below_kernel(
    inverse, share, code_ref, amp_ref, ens_above_ref, direction_above_ref, resid_above_ref,
    corr_ref, ens_ref, direction_ref, resid_ref, clim_ref, part_ref, back_ref,
    out_ref, sums_ref, scaled_ref, flat_ref, own_ref,
):
    count, patches, _ = ens_ref.shape
    patch_major(ens_ref, own_ref)
    patch_major(ens_above_ref, flat_ref)
    scale(flat_ref, direction_above_ref, resid_above_ref, scaled_ref)

    def body(b, _):
        start = b * BLOCK
        totals = gathered(
            scaled_ref, code_ref, (0, 1, 2), corr_ref, (0, 1, 2), amp_ref, start, BLOCK
        )
        for i in range(BLOCK):
            p = start + i
            first, second = contract(own_ref, p, totals[i], count)
            out_ref[0, pl.ds(p, 1), :] = first * inverse
            out_ref[1, pl.ds(p, 1), :] = second * inverse
        return 0

    lax.fori_loop(0, patches // BLOCK, body, 0)
    out_ref[...] = out_ref[...] + part_ref[...]
    clim = clim_ref[...] * share
    d = direction_ref[...]
    g = resid_ref[...]
    bottom = d * (out_ref[0] + clim * d) + direction_above_ref[...] * back_ref[0]
    top = g * (out_ref[1] + clim * g) + resid_above_ref[...] * back_ref[1]
    sums_ref[0:1, :] = jnp.sum(top, axis=0, keepdims=True)
    sums_ref[1:2, :] = jnp.sum(bottom, axis=0, keepdims=True)


def call(kernel, outs, scratch, args, specs, flops, moved):
    return pl.pallas_call(
        kernel,
        out_shape=outs,
        in_specs=specs,
        out_specs=jax.tree.map(lambda _: VMEM, outs),
        scratch_shapes=scratch,
        compiler_params=pltpu.CompilerParams(vmem_limit_bytes=24 * 1024 * 1024),
        cost_estimate=pl.CostEstimate(flops=flops, bytes_accessed=moved, transcendentals=0),
    )(*args)


def all_sum(values, axes, total):
    spread = jnp.broadcast_to(values[None], (total,) + values.shape)
    return jnp.sum(lax.all_to_all(spread, axes, 0, 0), axis=0)


def on_device(
    ens, direction, resid, increment, clim_var, corr_table, amp_table, adjacency, block_index
):
    count, patches, width = ens.shape
    groups = lax.axis_size("mem")
    tiles = lax.axis_size("tile")
    inverse = 1.0 / (count * groups - 1)
    rows = 2 * count
    classes = amp_table.shape[0]
    up = [(i, i + 1) for i in range(tiles - 1)]
    down = [(j, i) for i, j in up]

    code = (adjacency * classes + block_index).T
    code_above = lax.ppermute(code[6:9], "tile", up)
    if groups == 2:
        swap = [(0, 1), (1, 0)]
        lower = lax.axis_index("mem") == 0
        mine = lax.ppermute(jnp.where(lower, direction, resid), "tile", up)
        ens_above = lax.ppermute(ens, "tile", up)
        other = lax.ppermute(mine, "mem", swap)
        direction_above = jnp.where(lower, mine, other)
        resid_above = jnp.where(lower, other, mine)
    else:
        direction_above = lax.ppermute(direction, "tile", up)
        resid_above = lax.ppermute(resid, "tile", up)
        ens_above = lax.ppermute(ens, "tile", up)

    vec = jax.ShapeDtypeStruct((2, patches, width), F32)
    scaled_shape = (patches, rows, width)
    product = 6 * patches * rows * width * width
    part, scaled = call(
        functools.partial(own_kernel, inverse),
        (vec, jax.ShapeDtypeStruct(scaled_shape, BF16)),
        [flat_scratch(patches * count, width)],
        (code, amp_table, ens, direction, resid, corr_table),
        [SMEM, SMEM, VMEM, VMEM, VMEM, VMEM],
        product, 3000000,
    )
    upper = call(
        upper_kernel,
        jax.ShapeDtypeStruct((rows, patches, width), F32),
        [flat_scratch(patches * rows, width)],
        (code_above, amp_table, scaled, corr_table),
        [SMEM, SMEM, VMEM, VMEM],
        product, 3000000,
    )
    back = call(
        functools.partial(return_kernel, inverse), vec, [],
        (ens_above, upper), [VMEM, VMEM], 2 * rows * patches * width, 3000000,
    )
    returned = lax.ppermute(back, "tile", down)
    below, sums = call(
        functools.partial(below_kernel, inverse, 1.0 / groups),
        (vec, jax.ShapeDtypeStruct((2, width), F32)),
        [
            pltpu.VMEM(scaled_shape, BF16),
            flat_scratch(patches * count, width),
            flat_scratch(patches * count, width),
        ],
        (
            code, amp_table, ens_above, direction_above, resid_above, corr_table, ens,
            direction, resid, clim_var, part, back,
        ),
        [SMEM, SMEM] + [VMEM] * 10,
        product, 3000000,
    )
    sums = all_sum(jnp.sum(sums, axis=1), ("tile", "mem"), tiles * groups)
    partial_value = below + returned
    if groups == 2:
        total = partial_value + lax.ppermute(partial_value, "mem", swap)
    else:
        total = lax.psum(partial_value, "mem")
    applied_direction = total[0] + clim_var * direction
    applied_resid = total[1] + clim_var * resid
    step_size = sums[0] / sums[1]
    return (increment + step_size * applied_direction, applied_resid)


def solution(mesh):
    placed = (
        P("mem", "tile", None),
        P("tile", None),
        P("tile", None),
        P("tile", None),
        P("tile", None),
        P(),
        P(),
        P("tile", None),
        P("tile", None),
    )
    return jax.shard_map(
        on_device,
        mesh=mesh,
        in_specs=placed,
        out_specs=(P("tile", None), P("tile", None)),
        check_vma=False,
    )
```

time: 154 us -> 54.2 us (0.35)
  matrix products: 34.1 us -> 0 us
  waiting for transfers between devices: 32 us -> 0.02 us
  local copies, waits for them, and re-layouts: 22.9 us -> 1.95 us
  Pallas kernels: 0 us -> 18 us
  blocking collectives: 33.9 us -> 16.5 us
  between operations: 15.8 us -> 2.18 us
  starting transfers between devices: 5.42 us -> 12.4 us
  other arithmetic: 8.94 us -> 2.76 us
    dot_general x9 -> x0, matrix products: 34.1 us -> none  [neighbour_term(): jnp.dot(flattened, corr_table[slot_index], preferred_element_type=jnp.flo...]
    psum x1 -> x0, blocking collectives: 33.9 us -> none  [on_device(): lax.psum((jnp.sum(resid * applied[1]), jnp.sum(direction * applied[0])),...]
    psum x1 -> x0, waiting for transfers between devices: 32 us -> none  [on_device(): applied = lax.psum(partial_value, 'mem') + clim_var[None] * vectors]
    gather x9 -> x0, local copies, waits for them, and re-layouts: 18.3 us -> none  [neighbour_term(): picked = jnp.take(source, columns[:, slot_index], axis=1)]
    pallas_call x0 -> x4, Pallas kernels: none -> 18 us  [call(): pl.pallas_call(kernel, out_shape=outs, in_specs=specs, out_specs=jax.tree...]
    all_to_all x0 -> x1, blocking collectives: none -> 16.5 us  [all_sum(): return jnp.sum(lax.all_to_all(spread, axes, 0, 0), axis=0)]
    ppermute x2 -> x6, starting transfers between devices: 5.39 us -> 12.4 us  [the longest x1 4.48 us: on_device(): mine = lax.ppermute(jnp.where(lower, direction, resid), 'tile', up)]
    select_n x18 -> x2, other arithmetic: 4.65 us -> 0.97 us  [the longest x1 0.94 us: on_device(): mine = lax.ppermute(jnp.where(lower, direction, resid), 'tile', up)]
  transfers between devices with their start and end apart: 3 -> 6, of which waited for: 1 -> 0; matrix products, arithmetic and copies ran while one was open for 16% -> 7% of each run, Pallas kernels for 0% -> 33%
where the time goes in v1:
time: 54.2 us; the launch traced here: 53.8 us
  Pallas kernels  18 us (33%)
  blocking collectives  16.5 us (30%)
  starting transfers between devices  12.4 us (23%)
  other arithmetic  2.76 us (5%)
  between operations  2.18 us (4%)
  local copies, waits for them, and re-layouts  1.95 us (4%)
    pallas_call x4, Pallas kernels, call(): pl.pallas_call(kernel, out_shape=outs, in_specs=specs, out_specs=jax.tree...  18 us
    all_to_all x1, blocking collectives, all_sum(): return jnp.sum(lax.all_to_all(spread, axes, 0, 0), axis=0)  16.5 us
    ppermute x1, starting transfers between devices, on_device(): mine = lax.ppermute(jnp.where(lower, direction, resid), 'tile', up)  4.48 us
    ppermute x1, starting transfers between devices, on_device(): ens_above = lax.ppermute(ens, 'tile', up)  2.53 us
    ppermute x1, starting transfers between devices, on_device(): code_above = lax.ppermute(code[6:9], 'tile', up)  1.91 us
    ppermute x1, starting transfers between devices, on_device(): other = lax.ppermute(mine, 'mem', swap)  1.59 us
    ppermute x1, starting transfers between devices, on_device(): returned = lax.ppermute(back, 'tile', down)  1.29 us
    unnamed x13, local copies, waits for them, and re-layouts  1.23 us
  transfers between devices with their start and end apart: 6, of which 0 were waited for; matrix products, arithmetic and copies ran while one was open for 7% of the time, Pallas kernels for 33%

profile of v1, /device:TPU:0, one launch (start us, length us, event | category | flops | bytes accessed | tf_op | source)
XLA Modules:
  0.0 53.8 jit_solution(2577170643728260526)
XLA Ops:
  0.6 0.0 copy-start.1
  0.6 0.0 copy-start.2
  0.7 0.0 copy-start
  0.7 0.0 copy-start.4
  0.7 2.5 %collective-permute-start = (bf16[8,150,256]{2,0,1:T(8,128)(2,1)}, bf16[8,150,256]{2,0,1:T(8,128)(2,1)S(1)}, u32[]{:S(2)}, u32[]{:S(2)}) collective-permute-start(bf16[8,150,256]{2,0,1:T(8,128)(2,1)} %param.9), channel_id=1, source_target_pairs={{0,2},{2,4},{4,6},{6,8},{8,10},{10,12},{12,14},{14,16},{16,18},{18... | collective-permute-start | bytes 1843208 | tf_op jit(solution)/shard_map/ppermute | solution.py:201
  3.2 0.9 %broadcast_select_fusion.2 = f32[150,256]{1,0:T(8,128)S(1)} fusion(f32[150,256]{1,0:T(8,128)} %direction_ref.3, f32[150,256]{1,0:T(8,128)} %resid_ref.3, pred[]{:T(512)S(6)} %eq.3), kind=kLoop, calls=%fused_computation.8 | loop fusion | flops 38400 | bytes 460801 | tf_op jit(solution)/shard_map/jit(_where)/select_n | solution.py:200
  4.2 4.5 %collective-permute-start.1 = (f32[150,256]{1,0:T(8,128)S(1)}, f32[150,256]{1,0:T(8,128)S(1)}, u32[]{:S(2)}, u32[]{:S(2)}) collective-permute-start(f32[150,256]{1,0:T(8,128)S(1)} %broadcast_select_fusion.2), channel_id=1, source_target_pairs={{0,2},{2,4},{4,6},{6,8},{8,10},{10,12},{12,14},{14,16},{16,18},{18... | collective-permute-start | bytes 460808 | tf_op jit(solution)/shard_map/ppermute | solution.py:200
  8.6 0.7 %add_bitcast_fusion.code_ref = s32[9,150]{1,0:T(8,128)S(1)} fusion(s32[150,9]{0,1:T(8,128)} %param.17, s32[150,9]{0,1:T(8,128)} %param.16), kind=kLoop, calls=%fused_computation.9 | loop fusion | flops 2700 | bytes 16200 | tf_op jit(solution)/shard_map/transpose | solution.py:195
  9.4 1.9 %collective-permute-start.3 = (s32[3,150]{1,0:T(4,128)S(1)}, s32[3,150]{1,0:T(4,128)S(1)}, u32[]{:S(2)}, u32[]{:S(2)}) collective-permute-start(s32[3,150]{1,0:T(4,128)S(1)} %slice.20), channel_id=1, source_target_pairs={{0,2},{2,4},{4,6},{6,8},{8,10},{10,12},{12,14},{14,16},{16,18},{18... | collective-permute-start | bytes 5408 | tf_op jit(solution)/shard_map/ppermute | solution.py:196
  11.3 1.2 %copy.25.ens_ref = bf16[8,150,256]{2,1,0:T(8,128)(2,1)S(1)} copy(bf16[8,150,256]{2,0,1:T(8,128)(2,1)} %param.9) | data formatting | bytes 1228800 | tf_op args[0]
  12.5 0.0 collective-permute-done.1
  12.5 1.6 %collective-permute-start.2 = (f32[150,256]{1,0:T(8,128)S(1)}, f32[150,256]{1,0:T(8,128)S(1)}, u32[]{:S(2)}, u32[]{:S(2)}) collective-permute-start(f32[150,256]{1,0:T(8,128)S(1)} %collective-permute-done.1), channel_id=1, source_target_pairs={{0,1},{1,0},{2,3},{3,2},{4,5},{5,4},{6,7},{7,6},{8,9},{9,8},{10,11... | collective-permute-start | bytes 460808 | tf_op jit(solution)/shard_map/ppermute | solution.py:202
  14.1 0.0 copy-done.1
  14.1 0.0 copy-done.2
  14.1 0.0 copy-done
  14.1 0.0 copy-done.4
  14.1 6.0 %shard_map.104 = (f32[2,150,256]{2,1,0:T(8,128)S(1)}, bf16[150,16,256]{2,1,0:T(8,128)(2,1)S(1)}) custom-call(s32[9,150]{1,0:T(8,128)S(1)} %add_bitcast_fusion.code_ref, f32[16]{0:T(128)S(1)} %copy-done.4, bf16[8,150,256]{2,1,0:T(8,128)(2,1)S(1)} %copy.25.ens_ref, f32[150,256]{1,0:T(8,128)S(1)} %copy-done.1, f32[150,256]{1,0:T(8,128)S(1)} %copy-done.2, ...), custom_call_target="tpu_custom_call" | custom-call | flops 943718400 | bytes 3000000 | tf_op jit(solution)/shard_map/pallas_call | solution.py:167
  20.1 0.0 collective-permute-done.3.code_ref
  20.1 5.5 %shard_map.105.upper_ref = f32[16,150,256]{2,1,0:T(8,128)S(1)} custom-call(s32[3,150]{1,0:T(4,128)S(1)} %collective-permute-done.3.code_ref, f32[16]{0:T(128)S(1)} %copy-done.4, bf16[150,16,256]{2,1,0:T(8,128)(2,1)S(1)} %get-tuple-element.7.scaled_ref, bf16[9,256,256]{2,1,0:T(8,128)(2,1)S(1)} %copy-done), custom_call_target="tpu_custom_call" | custom-call | flops 943718400 | bytes 3000000 | tf_op jit(solution)/shard_map/pallas_call | solution.py:167
  25.6 0.0 collective-permute-done
  25.6 0.1 copy.24.ens_ref.ens_above_ref
  25.7 0.0 copy-start.3
  25.8 0.2 shard_map.106.back_ref
  26.0 1.3 %collective-permute-start.4 = (f32[2,150,256]{2,1,0:T(8,128)S(1)}, f32[2,150,256]{2,1,0:T(8,128)S(1)}, u32[]{:S(2)}, u32[]{:S(2)}) collective-permute-start(f32[2,150,256]{2,1,0:T(8,128)S(1)} %shard_map.106.back_ref), channel_id=1, source_target_pairs={{2,0},{4,2},{6,4},{8,6},{10,8},{12,10},{14,12},{16,14},{18,16},{20... | collective-permute-start | bytes 921608 | tf_op jit(solution)/shard_map/ppermute | solution.py:233
  27.3 0.0 collective-permute-done.2
  27.4 0.0 copy-done.3
  27.4 6.3 %shard_map.107 = (f32[2,150,256]{2,1,0:T(8,128)S(1)}, f32[2,256]{1,0:T(2,128)S(1)}) custom-call(s32[9,150]{1,0:T(8,128)S(1)} %add_bitcast_fusion.code_ref, f32[16]{0:T(128)S(1)} %copy-done.4, bf16[8,150,256]{2,1,0:T(8,128)(2,1)S(1)} %copy.24.ens_ref.ens_above_ref, f32[150,256]{1,0:T(8,128)S(1)} %get-tuple-element.13.direction_above_ref, ...), custom_call_target="tpu_custom_call" | custom-call | flops 943718400 | bytes 3000000 | tf_op jit(solution)/shard_map/pallas_call | solution.py:167
  33.7 0.0 copy-start.5
  33.7 0.0 collective-permute-done.4
  33.7 0.6 %collective-permute-start.5 = (f32[2,150,256]{2,1,0:T(8,128)S(1)}, f32[2,150,256]{2,1,0:T(8,128)S(1)}, u32[]{:S(2)}, u32[]{:S(2)}) collective-permute-start(f32[2,150,256]{2,1,0:T(8,128)S(1)} %add.19), channel_id=1, source_target_pairs={{0,1},{1,0},{2,3},{3,2},{4,5},{5,4},{6,7},{7,6},{8,9},{9,8},{10,11... | collective-permute-start | bytes 921608 | tf_op jit(solution)/shard_map/ppermute | solution.py:252
  34.3 0.1 reduce_sum.18
  34.4 16.5 %all_to_all.6 = f32[32,1,2]{2,1,0:T(1,128)S(1)} all-to-all(f32[32,1,2]{2,1,0:T(1,128)S(1)} %broadcast_in_dim.2), channel_id=1, replica_groups=mesh['tile'=16,'mem'=2] {'tile','mem'}, dimensions={0} | all-to-all | bytes 512 | tf_op jit(solution)/shard_map/all_to_all | solution.py:180
  50.9 0.1 reduce_sum.19
  51.0 0.6 %fusion.4 = (f32[1]{0:T(128)}, f32[1]{0:T(128)}) fusion(f32[2]{0:T(128)S(1)} %reduce_sum.19), kind=kLoop, calls=%fused_computation.10 | loop fusion | bytes 16 | tf_op jit(solution)/shard_map/slice | solution.py:257
  52.9 0.0 collective-permute-done.5
  52.9 0.0 copy-done.5
  53.0 0.8 %fusion = (f32[150,256]{1,0:T(8,128)}, f32[150,256]{1,0:T(8,128)}) fusion(f32[2,150,256]{2,1,0:T(8,128)S(1)} %add.20, f32[150,256]{1,0:T(8,128)S(1)} %copy-done.3, f32[150,256]{1,0:T(8,128)S(1)} %copy-done.2, f32[150,256]{1,0:T(8,128)S(1)} %copy-done.5, f32[150,256]{1,0:T(8,128)S(1)} %copy-done.1, f32[]{:T(128)} %bitcast.1), kind=kLoop, calls=%fused_computation.1 | loop fusion | flops 230400 | bytes 1228804 | tf_op jit(solution)/shard_map/add | solution.py:256
  (5 shorter events, 0.1 us)
Async XLA Ops:
  0.6 13.5 %copy-start.1 = (f32[150,256]{1,0:T(8,128)S(1)}, f32[150,256]{1,0:T(8,128)}, u32[]{:S(2)}) copy-start(f32[150,256]{1,0:T(8,128)} %direction_ref.3) | copy-start | bytes 460804
  0.6 13.5 %copy-start.2 = (f32[150,256]{1,0:T(8,128)S(1)}, f32[150,256]{1,0:T(8,128)}, u32[]{:S(2)}) copy-start(f32[150,256]{1,0:T(8,128)} %resid_ref.3) | copy-start | bytes 460804
  0.7 13.5 %copy-start = (bf16[9,256,256]{2,1,0:T(8,128)(2,1)S(1)}, bf16[9,256,256]{2,1,0:T(8,128)(2,1)}, u32[]{:S(2)}) copy-start(bf16[9,256,256]{2,1,0:T(8,128)(2,1)} %corr_ref.5) | copy-start | bytes 3538948
  0.7 13.5 %copy-start.4 = (f32[16]{0:T(128)S(1)}, f32[16]{0:T(128)}, u32[]{:S(2)}) copy-start(f32[16]{0:T(128)} %amp_ref.5) | copy-start | bytes 196
  0.7 24.9 %collective-permute-start = (bf16[8,150,256]{2,0,1:T(8,128)(2,1)}, bf16[8,150,256]{2,0,1:T(8,128)(2,1)S(1)}, u32[]{:S(2)}, u32[]{:S(2)}) collective-permute-start(bf16[8,150,256]{2,0,1:T(8,128)(2,1)} %param.9), channel_id=1, source_target_pairs={{0,2},{2,4},{4,6},{6,8},{8,10},{10,12},{12,14},{14,16},{16,18},{18... | collective-permute-start | bytes 1843208 | tf_op jit(solution)/shard_map/ppermute | solution.py:201
  4.2 8.4 %collective-permute-start.1 = (f32[150,256]{1,0:T(8,128)S(1)}, f32[150,256]{1,0:T(8,128)S(1)}, u32[]{:S(2)}, u32[]{:S(2)}) collective-permute-start(f32[150,256]{1,0:T(8,128)S(1)} %broadcast_select_fusion.2), channel_id=1, source_target_pairs={{0,2},{2,4},{4,6},{6,8},{8,10},{10,12},{12,14},{14,16},{16,18},{18... | collective-permute-start | bytes 460808 | tf_op jit(solution)/shard_map/ppermute | solution.py:200
  9.4 10.7 %collective-permute-start.3 = (s32[3,150]{1,0:T(4,128)S(1)}, s32[3,150]{1,0:T(4,128)S(1)}, u32[]{:S(2)}, u32[]{:S(2)}) collective-permute-start(s32[3,150]{1,0:T(4,128)S(1)} %slice.20), channel_id=1, source_target_pairs={{0,2},{2,4},{4,6},{6,8},{8,10},{10,12},{12,14},{14,16},{16,18},{18... | collective-permute-start | bytes 5408 | tf_op jit(solution)/shard_map/ppermute | solution.py:196
  12.5 14.8 %collective-permute-start.2 = (f32[150,256]{1,0:T(8,128)S(1)}, f32[150,256]{1,0:T(8,128)S(1)}, u32[]{:S(2)}, u32[]{:S(2)}) collective-permute-start(f32[150,256]{1,0:T(8,128)S(1)} %collective-permute-done.1), channel_id=1, source_target_pairs={{0,1},{1,0},{2,3},{3,2},{4,5},{5,4},{6,7},{7,6},{8,9},{9,8},{10,11... | collective-permute-start | bytes 460808 | tf_op jit(solution)/shard_map/ppermute | solution.py:202
  25.7 1.6 %copy-start.3 = (f32[150,256]{1,0:T(8,128)S(1)}, f32[150,256]{1,0:T(8,128)}, u32[]{:S(2)}) copy-start(f32[150,256]{1,0:T(8,128)} %clim_ref.1) | copy-start | bytes 460804
  26.0 7.7 %collective-permute-start.4 = (f32[2,150,256]{2,1,0:T(8,128)S(1)}, f32[2,150,256]{2,1,0:T(8,128)S(1)}, u32[]{:S(2)}, u32[]{:S(2)}) collective-permute-start(f32[2,150,256]{2,1,0:T(8,128)S(1)} %shard_map.106.back_ref), channel_id=1, source_target_pairs={{2,0},{4,2},{6,4},{8,6},{10,8},{12,10},{14,12},{16,14},{18,16},{20... | collective-permute-start | bytes 921608 | tf_op jit(solution)/shard_map/ppermute | solution.py:233
  33.7 19.3 %copy-start.5 = (f32[150,256]{1,0:T(8,128)S(1)}, f32[150,256]{1,0:T(8,128)}, u32[]{:S(2)}) copy-start(f32[150,256]{1,0:T(8,128)} %param.12) | copy-start | bytes 460804
  33.7 19.2 %collective-permute-start.5 = (f32[2,150,256]{2,1,0:T(8,128)S(1)}, f32[2,150,256]{2,1,0:T(8,128)S(1)}, u32[]{:S(2)}, u32[]{:S(2)}) collective-permute-start(f32[2,150,256]{2,1,0:T(8,128)S(1)} %add.19), channel_id=1, source_target_pairs={{0,1},{1,0},{2,3},{3,2},{4,5},{5,4},{6,7},{7,6},{8,9},{9,8},{10,11... | collective-permute-start | bytes 921608 | tf_op jit(solution)/shard_map/ppermute | solution.py:252

commit v2 on v0

v2 whole, which is shorter than its diff:
```python
import functools

import jax
import jax.numpy as jnp
from jax import lax
from jax.experimental import pallas as pl
from jax.experimental.pallas import tpu as pltpu
from jax.sharding import PartitionSpec as P

SLOTS = 9
BLOCK = 48
GROUP = 8
LANES = 128
F32 = jnp.float32
BF16 = jnp.bfloat16
VMEM = pl.BlockSpec(memory_space=pltpu.VMEM)
SENT_SCALE = 8192.0
SMEM = pl.BlockSpec(memory_space=pltpu.SMEM)


def blocks_of(patches):
    count = max(1, patches // BLOCK)
    starts = [i * BLOCK for i in range(count)] + [patches]
    return list(zip(starts[:-1], starts[1:]))


def scale(ens_ref, first_ref, second_ref, scaled_ref):
    patches = ens_ref.shape[0]

    def body(p, _):
        members = ens_ref[p].astype(F32)
        a = members * first_ref[pl.ds(p, 1), :]
        b = members * second_ref[pl.ds(p, 1), :]
        scaled_ref[p] = jnp.concatenate([a, b], axis=0).astype(BF16)
        return 0

    lax.fori_loop(0, patches, body, 0, unroll=10)


def gathered(
    scaled_ref, column_ref, class_ref, index_rows, corr_ref, slots, amp_ref, patches, skip=0
):
    rows = scaled_ref.shape[1]
    totals = None
    for row, slot in zip(index_rows, slots):
        left = jnp.concatenate([scaled_ref[column_ref[row, p]] for p in patches], axis=0)
        product = jnp.dot(left, corr_ref[slot], preferred_element_type=F32)
        weighted = [
            product[i * rows : (i + 1) * rows] * amp_ref[class_ref[skip + row, p]]
            for i, p in enumerate(patches)
        ]
        totals = weighted if totals is None else [t + w for t, w in zip(totals, weighted)]
    return totals


def member_sums(terms):
    count, width = terms[0].shape
    if count != GROUP:
        return jnp.concatenate([jnp.sum(t, axis=0, keepdims=True) for t in terms], axis=0)
    used = len(terms)
    terms = terms + [jnp.zeros((count, width), F32)] * (GROUP - used)
    place = lax.broadcasted_iota(jnp.int32, (count, width), 0)
    step = 1
    while len(terms) > 1:
        keep = (place & step) == 0
        terms = [
            jnp.where(keep, a, b) + pltpu.roll(jnp.where(keep, b, a), step, 0)
            for a, b in zip(terms[::2], terms[1::2])
        ]
        step *= 2
    return terms[0][:used]


def contract(ens_ref, out_ref, factor, patches, local):
    count = ens_ref.shape[1]
    for at in range(0, len(patches), GROUP):
        group = patches[at : at + GROUP]
        members = [ens_ref[p].astype(F32) for p in group]
        for v in range(2):
            terms = [
                e * local[at + i][v * count : (v + 1) * count] for i, e in enumerate(members)
            ]
            out_ref[v, group[0] : group[0] + len(group), :] = member_sums(terms) * factor


def first_kernel(amp_ref, out_ref):
    out_ref[...] = jnp.full(out_ref.shape, amp_ref[0], F32)


def load_kernel(
    first_ref, ens_ref, direction_ref, resid_ref, columns_ref, classes_ref, scaled_ref, sent_ref
):
    patches, width = direction_ref.shape
    padded = (sent_ref.shape[0] - GROUP) // 2
    sent_ref[2 * padded :, :] = jnp.zeros((GROUP, width), F32)
    sent_ref[2 * padded : 2 * padded + 3, :patches] = columns_ref[6:9, :].astype(F32)
    sent_ref[2 * padded + 3 : 2 * padded + 6, :patches] = classes_ref[6:9, :].astype(F32)
    sent_ref[:patches, :] = direction_ref[...] * SENT_SCALE
    sent_ref[padded : padded + patches, :] = resid_ref[...] * SENT_SCALE
    scale(ens_ref, direction_ref, resid_ref, scaled_ref)


def own_kernel(
    inverse, column_ref, class_ref, amp_ref, scaled_ref, ens_ref, corr_ref, part_ref
):
    for start, end in blocks_of(ens_ref.shape[0]):
        patches = list(range(start, end))
        slots = (3, 4, 5)
        totals = gathered(
            scaled_ref, column_ref, class_ref, slots, corr_ref, slots, amp_ref, patches
        )
        local = [t + scaled_ref[p].astype(F32) for t, p in zip(totals, patches)]
        contract(ens_ref, part_ref, inverse, patches, local)


def upper_kernel(index_ref, amp_ref, scaled_ref, corr_ref, out_ref):
    for start, end in blocks_of(scaled_ref.shape[0]):
        patches = list(range(start, end))
        totals = gathered(
            scaled_ref, index_ref, index_ref, (0, 1, 2), corr_ref, (6, 7, 8), amp_ref, patches, 3
        )
        for t, p in zip(totals, patches):
            out_ref[p] = t


def back_kernel(inverse, ens_ref, upper_ref, out_ref):
    for start, end in blocks_of(ens_ref.shape[0]):
        patches = list(range(start, end))
        contract(ens_ref, out_ref, inverse, patches, [upper_ref[p] for p in patches])


def below_kernel(
    inverse, share, column_ref, class_ref, amp_ref, ens_above_ref, above_ref,
    corr_ref, ens_ref, direction_ref, resid_ref, clim_ref, part_ref, back_ref,
    out_ref, sums_ref, scaled_ref,
):
    patches = ens_ref.shape[0]
    padded = (above_ref.shape[0] - GROUP) // 2
    direction_above_ref = above_ref.at[:padded]
    resid_above_ref = above_ref.at[padded : 2 * padded]
    scale(ens_above_ref, direction_above_ref, resid_above_ref, scaled_ref)
    for start, end in blocks_of(patches):
        block = list(range(start, end))
        slots = (0, 1, 2)
        totals = gathered(
            scaled_ref, column_ref, class_ref, slots, corr_ref, slots, amp_ref, block
        )
        contract(ens_ref, out_ref, inverse, block, totals)
    out_ref[...] = out_ref[...] + part_ref[...]
    clim = clim_ref[...] * share
    d = direction_ref[...]
    g = resid_ref[...]
    bottom = d * (out_ref[0] + clim * d) + direction_above_ref[:patches, :] * back_ref[0]
    top = g * (out_ref[1] + clim * g) + resid_above_ref[:patches, :] * back_ref[1]
    place = lax.broadcasted_iota(jnp.int32, sums_ref.shape, 2)
    sums_ref[...] = jnp.where(place == 0, jnp.sum(top), jnp.sum(bottom))


def final_kernel(
    sums_ref, mine_ref, other_ref, clim_ref, direction_ref, resid_ref, increment_ref,
    new_ref, precond_ref,
):
    sums = jnp.sum(sums_ref[...], axis=0)
    step = sums[:, 0:1] / sums[:, 1:2]
    clim = clim_ref[...]
    first = mine_ref[0] + other_ref[0] + clim * direction_ref[...]
    new_ref[...] = increment_ref[...] + step * first
    precond_ref[...] = mine_ref[1] + other_ref[1] + clim * resid_ref[...]


def call(kernel, outs, scratch, args, specs, flops, moved):
    return pl.pallas_call(
        kernel,
        out_shape=outs,
        in_specs=specs,
        out_specs=jax.tree.map(lambda _: VMEM, outs),
        scratch_shapes=scratch,
        compiler_params=pltpu.CompilerParams(vmem_limit_bytes=24 * 1024 * 1024),
        cost_estimate=pl.CostEstimate(flops=flops, bytes_accessed=moved, transcendentals=0),
    )(*args)


def on_device(
    ens, direction, resid, increment, clim_var, corr_table, amp_table, adjacency, block_index
):
    count, patches, width = ens.shape
    groups = lax.axis_size("mem")
    tiles = lax.axis_size("tile")
    inverse = 1.0 / (count * groups - 1)
    rows = 2 * count
    up = [(i, i + 1) for i in range(tiles - 1)]
    down = [(j, i) for i, j in up]
    padded = patches + (-patches % GROUP)
    columns = adjacency.T
    classes = block_index.T

    vec = jax.ShapeDtypeStruct((2, patches, width), F32)
    flat = jax.ShapeDtypeStruct((patches, width), F32)
    local_shape = (patches, rows, width)
    product = 6 * patches * rows * width * width

    ens = jnp.transpose(ens, (1, 0, 2))
    ens_above = lax.ppermute(ens, "tile", up)
    first = call(
        first_kernel,
        jax.ShapeDtypeStruct((GROUP, LANES), F32),
        [],
        (amp_table,),
        [SMEM],
        4000000000, 30000000,
    )
    scaled, sent = call(
        load_kernel,
        (
            jax.ShapeDtypeStruct(local_shape, BF16),
            jax.ShapeDtypeStruct((2 * padded + GROUP, width), F32),
        ),
        [],
        (first, ens, direction, resid, columns, classes),
        [VMEM] * 6,
        rows * patches * width, 3000000,
    )
    above = lax.ppermute(sent.astype(jnp.float16), "tile", up).astype(F32)
    index_above = above[2 * padded : 2 * padded + 6, :patches].astype(jnp.int32)
    above = above * (1.0 / SENT_SCALE)
    part = call(
        functools.partial(own_kernel, inverse),
        vec,
        [],
        (columns, classes, amp_table, scaled, ens, corr_table),
        [SMEM, SMEM, SMEM, VMEM, VMEM, VMEM],
        product, 3000000,
    )
    upper = call(
        upper_kernel,
        jax.ShapeDtypeStruct(local_shape, F32),
        [],
        (index_above, amp_table, scaled, corr_table),
        [SMEM, SMEM, VMEM, VMEM],
        product, 3000000,
    )
    back = call(
        functools.partial(back_kernel, inverse), vec, [],
        (ens_above, upper), [VMEM, VMEM], 2 * rows * patches * width, 3000000,
    )
    returned = lax.ppermute(back, "tile", down)
    below, sums = call(
        functools.partial(below_kernel, inverse, 1.0 / groups),
        (vec, jax.ShapeDtypeStruct((tiles * groups, 1, 2), F32)),
        [pltpu.VMEM(local_shape, BF16)],
        (
            columns, classes, amp_table, ens_above, above, corr_table, ens,
            direction, resid, clim_var, part, back,
        ),
        [SMEM] * 3 + [VMEM] * 9,
        product, 3000000,
    )
    mine = below + returned
    if groups == 2:
        other = lax.ppermute(mine, "mem", [(0, 1), (1, 0)])
    else:
        other = lax.psum(mine, "mem")
        mine = jnp.zeros_like(mine)
    sums = lax.all_to_all(sums, ("tile", "mem"), 0, 0)
    return call(
        final_kernel, (flat, flat), [],
        (sums, mine, other, clim_var, direction, resid, increment),
        [VMEM] * 7, 20 * patches * width, 3000000,
    )


def solution(mesh):
    placed = (
        P("mem", "tile", None),
        P("tile", None),
        P("tile", None),
        P("tile", None),
        P("tile", None),
        P(),
        P(),
        P("tile", None),
        P("tile", None),
    )
    return jax.shard_map(
        on_device,
        mesh=mesh,
        in_specs=placed,
        out_specs=(P("tile", None), P("tile", None)),
        check_vma=False,
    )
```

time: 154 us -> 39.9 us (0.26)
  matrix products: 34.1 us -> 0 us
  waiting for transfers between devices: 32 us -> 1.24 us
  local copies, waits for them, and re-layouts: 22.9 us -> 0.7 us
  blocking collectives: 33.9 us -> 17.1 us
  between operations: 15.8 us -> 0.89 us
  Pallas kernels: 0 us -> 9.73 us
  other arithmetic: 8.94 us -> 0.12 us
  starting transfers between devices: 5.42 us -> 9.88 us
    dot_general x9 -> x0, matrix products: 34.1 us -> none  [neighbour_term(): jnp.dot(flattened, corr_table[slot_index], preferred_element_type=jnp.flo...]
    psum x1 -> x0, blocking collectives: 33.9 us -> none  [on_device(): lax.psum((jnp.sum(resid * applied[1]), jnp.sum(direction * applied[0])),...]
    psum x1 -> x0, waiting for transfers between devices: 32 us -> none  [on_device(): applied = lax.psum(partial_value, 'mem') + clim_var[None] * vectors]
    gather x9 -> x0, local copies, waits for them, and re-layouts: 18.3 us -> none  [neighbour_term(): picked = jnp.take(source, columns[:, slot_index], axis=1)]
    all_to_all x0 -> x1, blocking collectives: none -> 17.1 us  [on_device(): sums = lax.all_to_all(sums, ('tile', 'mem'), 0, 0)]
    pallas_call x0 -> x7, Pallas kernels: none -> 9.73 us  [call(): pl.pallas_call(kernel, out_shape=outs, in_specs=specs, out_specs=jax.tree...]
    select_n x18 -> x0, other arithmetic: 4.65 us -> none  [neighbour_term(): picked = jnp.take(source, columns[:, slot_index], axis=1)]
    ppermute x2 -> x4, starting transfers between devices: 5.39 us -> 9.88 us  [the longest x1 4.48 us: on_device(): above = lax.ppermute(sent.astype(jnp.float16), 'tile', up).astype(F32)]
  transfers between devices with their start and end apart: 3 -> 4, of which waited for: 1 -> 1; matrix products, arithmetic and copies ran while one was open for 16% -> 0% of each run, Pallas kernels for 0% -> 21%
where the time goes in v2:
time: 39.9 us; the launch traced here: 39.7 us
  blocking collectives  17.1 us (43%)
  starting transfers between devices  9.88 us (25%)
  Pallas kernels  9.73 us (24%)
  waiting for transfers between devices  1.24 us (3%)
  between operations  0.89 us (2%)
  local copies, waits for them, and re-layouts  0.7 us (2%)
    all_to_all x1, blocking collectives, on_device(): sums = lax.all_to_all(sums, ('tile', 'mem'), 0, 0)  17.1 us
    pallas_call x7, Pallas kernels, call(): pl.pallas_call(kernel, out_shape=outs, in_specs=specs, out_specs=jax.tree...  9.73 us
    ppermute x1, starting transfers between devices, on_device(): above = lax.ppermute(sent.astype(jnp.float16), 'tile', up).astype(F32)  4.48 us
    ppermute x1, starting transfers between devices, on_device(): ens_above = lax.ppermute(ens, 'tile', up)  2.53 us
    ppermute x1, starting transfers between devices, on_device(): other = lax.ppermute(mine, 'mem', [(0, 1), (1, 0)])  1.58 us
    ppermute x1, starting transfers between devices, on_device(): returned = lax.ppermute(back, 'tile', down)  1.29 us
    ppermute x1, waiting for transfers between devices, on_device(): returned = lax.ppermute(back, 'tile', down)  1.24 us
  transfers between devices with their start and end apart: 4, of which 1 were waited for; matrix products, arithmetic and copies ran while one was open for 0% of the time, Pallas kernels for 21%

profile of v2, /device:TPU:0, one launch (start us, length us, event | category | flops | bytes accessed | tf_op | source)
XLA Modules:
  0.0 39.7 jit_solution(15671438058416667465)
XLA Ops:
  0.6 0.0 copy-start.1
  0.6 0.0 copy-start.2
  0.7 0.0 copy-start.3
  0.7 0.0 copy-start.6
  0.7 0.0 copy-start.7
  0.7 2.5 %collective-permute-start = (bf16[150,8,256]{2,1,0:T(8,128)(2,1)}, bf16[150,8,256]{2,1,0:T(8,128)(2,1)S(1)}, u32[]{:S(2)}, u32[]{:S(2)}) collective-permute-start(bf16[150,8,256]{2,1,0:T(8,128)(2,1)} %bitcast.3), channel_id=1, source_target_pairs={{0,2},{2,4},{4,6},{6,8},{8,10},{10,12},{12,14},{14,16},{16,18},{18... | collective-permute-start | bytes 1843208 | tf_op jit(solution)/shard_map/ppermute | solution.py:203
  3.2 0.0 copy-start.8
  3.2 0.6 %copy-done.8 = f32[16]{0:T(128)S(1)} copy-done((f32[16]{0:T(128)S(1)}, f32[16]{0:T(128)}, u32[]{:S(2)}) %copy-start.8) | copy-done | bytes 88
  3.9 0.5 %shard_map.104.first_ref = f32[8,128]{1,0:T(8,128)S(1)} custom-call(f32[16]{0:T(128)S(1)} %copy-done.8), custom_call_target="tpu_custom_call" | custom-call | flops 4000000000 | bytes 30000000 | tf_op jit(solution)/shard_map/pallas_call | solution.py:172
  4.4 0.0 copy-start
  4.4 0.0 copy-done.1
  4.4 0.0 copy-done.2
  4.5 0.0 copy-done.3
  4.5 0.0 copy-done.6
  4.5 0.0 copy-done.7
  4.5 0.4 shard_map.105
  4.9 4.5 %collective-permute-start.1 = (f16[312,256]{1,0:T(8,128)(2,1)S(1)}, f16[312,256]{1,0:T(8,128)(2,1)S(1)}, u32[]{:S(2)}, u32[]{:S(2)}) collective-permute-start(f16[312,256]{1,0:T(8,128)(2,1)S(1)} %convert_element_type.9), channel_id=1, source_target_pairs={{0,2},{2,4},{4,6},{6,8},{8,10},{10,12},{12,14},{14,16},{16,18},{18... | collective-permute-start | bytes 479240 | tf_op jit(solution)/shard_map/ppermute | solution.py:223
  9.4 0.0 copy-done
  9.4 0.0 copy-start.9
  9.4 2.7 %shard_map.106.part_ref = f32[2,150,256]{2,1,0:T(8,128)S(1)} custom-call(s32[9,150]{1,0:T(8,128)S(1)} %bitcast.8, s32[9,150]{1,0:T(8,128)S(1)} %bitcast.11, f32[16]{0:T(128)S(1)} %copy-done.8, bf16[150,16,256]{2,1,0:T(8,128)(2,1)S(1)} %get-tuple-element.7.scaled_ref, bf16[150,8,256]{2,1,0:T(8,128)(2,1)S(1)} %bitcast.5, bf16[9,256,256]{2,1,0:T(8,128)(2,1)S(1)} %copy-done), custom_call_target="tpu_custom_call" | custom-call | flops 943718400 | bytes 3000000 | tf_op jit(solution)/shard_map/pallas_call | solution.py:172
  12.1 0.0 collective-permute-done.1
  12.1 0.0 copy-done.9
  12.2 1.8 %shard_map.107.upper_ref = f32[150,16,256]{2,1,0:T(8,128)S(1)} custom-call(s32[6,150]{1,0:T(8,128)S(1)} %slice_convert_fusion.index_ref, f32[16]{0:T(128)S(1)} %copy-done.9, bf16[150,16,256]{2,1,0:T(8,128)(2,1)S(1)} %get-tuple-element.7.scaled_ref, bf16[9,256,256]{2,1,0:T(8,128)(2,1)S(1)} %copy-done), custom_call_target="tpu_custom_call" | custom-call | flops 943718400 | bytes 3000000 | tf_op jit(solution)/shard_map/pallas_call | solution.py:172
  14.0 0.0 copy-start.4
  14.0 0.0 collective-permute-done.ens_ref.ens_above_ref
  14.0 0.4 %shard_map.108.back_ref = f32[2,150,256]{2,1,0:T(8,128)S(1)} custom-call(bf16[150,8,256]{2,1,0:T(8,128)(2,1)S(1)} %collective-permute-done.ens_ref.ens_above_ref, f32[150,16,256]{2,1,0:T(8,128)S(1)} %shard_map.107.upper_ref), custom_call_target="tpu_custom_call" | custom-call | flops 1228800 | bytes 3000000 | tf_op jit(solution)/shard_map/pallas_call | solution.py:172
  14.5 1.3 %collective-permute-start.2 = (f32[2,150,256]{2,1,0:T(8,128)S(1)}, f32[2,150,256]{2,1,0:T(8,128)S(1)}, u32[]{:S(2)}, u32[]{:S(2)}) collective-permute-start(f32[2,150,256]{2,1,0:T(8,128)S(1)} %shard_map.108.back_ref), channel_id=1, source_target_pairs={{2,0},{4,2},{6,4},{8,6},{10,8},{12,10},{14,12},{16,14},{18,16},{20... | collective-permute-start | bytes 921608 | tf_op jit(solution)/shard_map/ppermute | solution.py:246
  15.8 0.0 copy-done.4
  15.8 0.0 copy-start.5
  15.8 3.0 %shard_map.109 = (f32[2,150,256]{2,1,0:T(8,128)S(1)}, f32[32,1,2]{2,1,0:T(1,128)S(1)}) custom-call(s32[9,150]{1,0:T(8,128)S(1)} %bitcast.9, s32[9,150]{1,0:T(8,128)S(1)} %bitcast.12, f32[16]{0:T(128)S(1)} %copy-done.9, bf16[150,8,256]{2,1,0:T(8,128)(2,1)S(1)} %collective-permute-done.ens_ref.ens_above_ref, f32[312,256]{1,0:T(8,128)S(1)} %broadcast_multiply_fusion.above_ref, ...), custom_call_target="tpu_custom_call" | custom-call | flops 943718400 | bytes 3000000 | tf_op jit(solution)/shard_map/pallas_call | solution.py:172
  18.9 1.2 %collective-permute-done.2 = f32[2,150,256]{2,1,0:T(8,128)S(1)} collective-permute-done((f32[2,150,256]{2,1,0:T(8,128)S(1)}, f32[2,150,256]{2,1,0:T(8,128)S(1)}, u32[]{:S(2)}, u32[]{:S(2)}) %collective-permute-start.2) | collective-permute-done | bytes 307232 | tf_op jit(solution)/shard_map/ppermute | solution.py:246
  20.1 1.6 %collective-permute-start.3 = (f32[2,150,256]{2,1,0:T(8,128)S(1)}, f32[2,150,256]{2,1,0:T(8,128)S(1)}, u32[]{:S(2)}, u32[]{:S(2)}) collective-permute-start(f32[2,150,256]{2,1,0:T(8,128)S(1)} %add.3.mine_ref), channel_id=1, source_target_pairs={{0,1},{1,0},{2,3},{3,2},{4,5},{5,4},{6,7},{7,6},{8,9},{9,8},{10,11... | collective-permute-start | bytes 921608 | tf_op jit(solution)/shard_map/ppermute | solution.py:260
  21.7 17.1 %all_to_all.5.sums_ref = f32[32,1,2]{2,1,0:T(1,128)S(1)} all-to-all(f32[32,1,2]{2,1,0:T(1,128)S(1)} %get-tuple-element.8), channel_id=1, replica_groups=mesh['tile'=16,'mem'=2] {'tile','mem'}, dimensions={0} | all-to-all | bytes 512 | tf_op jit(solution)/shard_map/all_to_all | solution.py:264
  38.9 0.0 collective-permute-done.3.other_ref
  38.9 0.0 copy-done.5
  38.9 0.8 %shard_map.110 = (f32[150,256]{1,0:T(8,128)}, f32[150,256]{1,0:T(8,128)}) custom-call(f32[32,1,2]{2,1,0:T(1,128)S(1)} %all_to_all.5.sums_ref, f32[2,150,256]{2,1,0:T(8,128)S(1)} %add.3.mine_ref, f32[2,150,256]{2,1,0:T(8,128)S(1)} %collective-permute-done.3.other_ref, f32[150,256]{1,0:T(8,128)S(1)} %copy-done.4, f32[150,256]{1,0:T(8,128)S(1)} %copy-done.2, ...), custom_call_target="tpu_custom_call" | custom-call | flops 768000 | bytes 3000000 | tf_op jit(solution)/shard_map/pallas_call | solution.py:172
  (5 shorter events, 0.1 us)
Async XLA Ops:
  0.6 3.8 %copy-start.1 = (bf16[8,150,256]{2,0,1:T(8,128)(2,1)S(1)}, bf16[8,150,256]{2,0,1:T(8,128)(2,1)}, u32[]{:S(2)}) copy-start(bf16[8,150,256]{2,0,1:T(8,128)(2,1)} %param.9) | copy-start | bytes 1843204
  0.6 3.8 %copy-start.2 = (f32[150,256]{1,0:T(8,128)S(1)}, f32[150,256]{1,0:T(8,128)}, u32[]{:S(2)}) copy-start(f32[150,256]{1,0:T(8,128)} %direction_ref.5) | copy-start | bytes 460804
  0.7 3.8 %copy-start.3 = (f32[150,256]{1,0:T(8,128)S(1)}, f32[150,256]{1,0:T(8,128)}, u32[]{:S(2)}) copy-start(f32[150,256]{1,0:T(8,128)} %resid_ref.5) | copy-start | bytes 460804
  0.7 3.8 %copy-start.6 = (s32[150,9]{0,1:T(8,128)S(1)}, s32[150,9]{0,1:T(8,128)}, u32[]{:S(2)}) copy-start(s32[150,9]{0,1:T(8,128)} %param.16) | copy-start | bytes 16204
  0.7 3.8 %copy-start.7 = (s32[150,9]{0,1:T(8,128)S(1)}, s32[150,9]{0,1:T(8,128)}, u32[]{:S(2)}) copy-start(s32[150,9]{0,1:T(8,128)} %param.17) | copy-start | bytes 16204
  0.7 13.3 %collective-permute-start = (bf16[150,8,256]{2,1,0:T(8,128)(2,1)}, bf16[150,8,256]{2,1,0:T(8,128)(2,1)S(1)}, u32[]{:S(2)}, u32[]{:S(2)}) collective-permute-start(bf16[150,8,256]{2,1,0:T(8,128)(2,1)} %bitcast.3), channel_id=1, source_target_pairs={{0,2},{2,4},{4,6},{6,8},{8,10},{10,12},{12,14},{14,16},{16,18},{18... | collective-permute-start | bytes 1843208 | tf_op jit(solution)/shard_map/ppermute | solution.py:203
  3.2 0.7 %copy-start.8 = (f32[16]{0:T(128)S(1)}, f32[16]{0:T(128)}, u32[]{:S(2)}) copy-start(f32[16]{0:T(128)} %amp_ref.7) | copy-start | bytes 196
  4.4 5.0 %copy-start = (bf16[9,256,256]{2,1,0:T(8,128)(2,1)S(1)}, bf16[9,256,256]{2,1,0:T(8,128)(2,1)}, u32[]{:S(2)}) copy-start(bf16[9,256,256]{2,1,0:T(8,128)(2,1)} %corr_ref.5) | copy-start | bytes 3538948
  4.9 7.2 %collective-permute-start.1 = (f16[312,256]{1,0:T(8,128)(2,1)S(1)}, f16[312,256]{1,0:T(8,128)(2,1)S(1)}, u32[]{:S(2)}, u32[]{:S(2)}) collective-permute-start(f16[312,256]{1,0:T(8,128)(2,1)S(1)} %convert_element_type.9), channel_id=1, source_target_pairs={{0,2},{2,4},{4,6},{6,8},{8,10},{10,12},{12,14},{14,16},{16,18},{18... | collective-permute-start | bytes 479240 | tf_op jit(solution)/shard_map/ppermute | solution.py:223
  9.4 2.7 %copy-start.9 = (f32[16]{0:T(128)S(1)}, f32[16]{0:T(128)}, u32[]{:S(2)}) copy-start(f32[16]{0:T(128)} %amp_ref.7) | copy-start | bytes 196
  14.0 1.8 %copy-start.4 = (f32[150,256]{1,0:T(8,128)S(1)}, f32[150,256]{1,0:T(8,128)}, u32[]{:S(2)}) copy-start(f32[150,256]{1,0:T(8,128)} %clim_ref.3) | copy-start | bytes 460804
  14.5 5.6 %collective-permute-start.2 = (f32[2,150,256]{2,1,0:T(8,128)S(1)}, f32[2,150,256]{2,1,0:T(8,128)S(1)}, u32[]{:S(2)}, u32[]{:S(2)}) collective-permute-start(f32[2,150,256]{2,1,0:T(8,128)S(1)} %shard_map.108.back_ref), channel_id=1, source_target_pairs={{2,0},{4,2},{6,4},{8,6},{10,8},{12,10},{14,12},{16,14},{18,16},{20... | collective-permute-start | bytes 921608 | tf_op jit(solution)/shard_map/ppermute | solution.py:246
  15.8 23.1 %copy-start.5 = (f32[150,256]{1,0:T(8,128)S(1)}, f32[150,256]{1,0:T(8,128)}, u32[]{:S(2)}) copy-start(f32[150,256]{1,0:T(8,128)} %increment_ref.1) | copy-start | bytes 460804
  20.1 18.7 %collective-permute-start.3 = (f32[2,150,256]{2,1,0:T(8,128)S(1)}, f32[2,150,256]{2,1,0:T(8,128)S(1)}, u32[]{:S(2)}, u32[]{:S(2)}) collective-permute-start(f32[2,150,256]{2,1,0:T(8,128)S(1)} %add.3.mine_ref), channel_id=1, source_target_pairs={{0,1},{1,0},{2,3},{3,2},{4,5},{5,4},{6,7},{7,6},{8,9},{9,8},{10,11... | collective-permute-start | bytes 921608 | tf_op jit(solution)/shard_map/ppermute | solution.py:260

commit v3 on v2

v3 whole, which is shorter than its diff:
```python
import functools
import math

import jax
import jax.numpy as jnp
from jax import lax
from jax.experimental import pallas as pl
from jax.experimental.pallas import tpu as pltpu
from jax.sharding import PartitionSpec as P

SLOTS = 9
BLOCK = 48
GROUP = 8
LANES = 128
F32 = jnp.float32
BF16 = jnp.bfloat16
VMEM = pl.BlockSpec(memory_space=pltpu.VMEM)
SENT_BITS = 15
ANY = pl.BlockSpec(memory_space=pl.ANY)


def blocks_of(patches):
    count = max(1, patches // BLOCK)
    starts = [i * BLOCK for i in range(count)] + [patches]
    return list(zip(starts[:-1], starts[1:]))


def scale(ens_ref, first_at, second_at, scaled_ref):
    patches = ens_ref.shape[0]

    def body(p, _):
        members = ens_ref[p].astype(F32)
        a = members * first_at[pl.ds(p, 1), :][...]
        b = members * second_at[pl.ds(p, 1), :][...]
        scaled_ref[p] = jnp.concatenate([a, b], axis=0).astype(BF16)
        return 0

    lax.fori_loop(0, patches, body, 0, unroll=10)


def gathered(
    scaled_ref, column_ref, class_ref, index_rows, corr_ref, slots, amp_ref, patches, skip=0
):
    rows = scaled_ref.shape[1]
    totals = None
    for row, slot in zip(index_rows, slots):
        left = jnp.concatenate([scaled_ref[column_ref[row, p]] for p in patches], axis=0)
        product = jnp.dot(left, corr_ref[slot], preferred_element_type=F32)
        weighted = [
            product[i * rows : (i + 1) * rows] * amp_ref[class_ref[skip + row, p]]
            for i, p in enumerate(patches)
        ]
        totals = weighted if totals is None else [t + w for t, w in zip(totals, weighted)]
    return totals


def member_sums(terms):
    count, width = terms[0].shape
    if count != GROUP:
        return jnp.concatenate([jnp.sum(t, axis=0, keepdims=True) for t in terms], axis=0)
    used = len(terms)
    terms = terms + [jnp.zeros((count, width), F32)] * (GROUP - used)
    place = lax.broadcasted_iota(jnp.int32, (count, width), 0)
    step = 1
    while len(terms) > 1:
        keep = (place & step) == 0
        terms = [
            jnp.where(keep, a, b) + pltpu.roll(jnp.where(keep, b, a), step, 0)
            for a, b in zip(terms[::2], terms[1::2])
        ]
        step *= 2
    return terms[0][:used]


def contract(ens_ref, out_ref, factors, patches, local):
    count = ens_ref.shape[1]
    for at in range(0, len(patches), GROUP):
        group = patches[at : at + GROUP]
        members = [ens_ref[p].astype(F32) for p in group]
        for v in range(2):
            terms = [
                e * local[at + i][v * count : (v + 1) * count] for i, e in enumerate(members)
            ]
            out_ref[v, group[0] : group[0] + len(group), :] = member_sums(terms) * factors[v]


def first_kernel(out_ref):
    out_ref[...] = jnp.zeros(out_ref.shape, F32)


def started(sources, targets, sems):
    copies = [
        pltpu.make_async_copy(source, target, sems.at[i])
        for i, (source, target) in enumerate(zip(sources, targets))
    ]
    for copy in copies:
        copy.start()
    return copies


def note_kernel(first_ref, direction_ref, resid_ref, columns_ref, classes_ref, note_ref):
    patches, width = direction_ref.shape
    note_ref[...] = jnp.zeros(note_ref.shape, F32)
    note_ref[0:3, :patches] = columns_ref[6:9, :].astype(F32)
    note_ref[3:6, :patches] = classes_ref[6:9, :].astype(F32)
    for v, vector_ref in enumerate((direction_ref, resid_ref)):
        largest = jnp.max(jnp.abs(vector_ref[...]), axis=0, keepdims=True)
        largest = jnp.maximum(jnp.max(largest, axis=1, keepdims=True), 1e-30)
        exponent = jnp.floor(jnp.log(largest) * (1.0 / math.log(2.0))) + 1.0
        note_ref[6 + v : 7 + v, :] = jnp.broadcast_to(exponent, (1, width))


def own_kernel(
    inverse, columns_any, classes_any, amp_any, note_ref, ens_ref, direction_ref, resid_ref,
    corr_ref, part_ref, scaled_ref, sent_ref, column_ref, class_ref, amp_ref, sems,
):
    copies = started(
        (columns_any, classes_any, amp_any), (column_ref, class_ref, amp_ref), sems
    )
    patches, width = direction_ref.shape
    padded = sent_ref.shape[0] // 2
    for v, vector_ref in enumerate((direction_ref, resid_ref)):
        at = v * padded
        factor = jnp.exp2(SENT_BITS - note_ref[6 + v : 7 + v, :])
        sent_ref[at : at + patches, :] = vector_ref[...] * factor
        if padded > patches:
            sent_ref[at + patches : at + padded, :] = jnp.zeros((padded - patches, width), F32)
    scale(ens_ref, direction_ref.at, resid_ref.at, scaled_ref)
    for copy in copies:
        copy.wait()
    slots = (3, 4, 5)
    for start, end in blocks_of(patches):
        block = list(range(start, end))
        totals = gathered(
            scaled_ref, column_ref, class_ref, slots, corr_ref, slots, amp_ref, block
        )
        local = [t + scaled_ref[p].astype(F32) for t, p in zip(totals, block)]
        contract(ens_ref, part_ref, [inverse, inverse], block, local)


def back_kernel(
    unit, index_any, amp_any, note_ref, ens_ref, scaled_ref, corr_ref, out_ref,
    products_ref, index_ref, amp_ref, sems,
):
    copies = started((index_any, amp_any), (index_ref, amp_ref), sems)
    patches, rows, width = scaled_ref.shape
    for start, end in blocks_of(patches):
        left = scaled_ref[start:end].reshape((end - start) * rows, width)
        for i in range(3):
            product = jnp.dot(left, corr_ref[6 + i], preferred_element_type=F32)
            products_ref[i, start:end] = product.reshape(end - start, rows, width)
    factors = [jnp.exp2(-note_ref[6 + v : 7 + v, :]) * (1.0 / unit) for v in range(2)]
    for v in range(2):
        out_ref[v, patches:, :] = jnp.broadcast_to(
            note_ref[6 + v : 7 + v, :], (out_ref.shape[1] - patches, width)
        )
    for copy in copies:
        copy.wait()
    for start, end in blocks_of(patches):
        block = list(range(start, end))
        local = [
            sum(
                products_ref[i, index_ref[i, p]] * amp_ref[index_ref[3 + i, p]] for i in range(3)
            )
            for p in block
        ]
        contract(ens_ref, out_ref, factors, block, local)


def below_kernel(
    inverse, share, unit, columns_any, classes_any, amp_any, ens_above_ref, above_ref,
    note_above_ref, note_ref, corr_ref, ens_ref, direction_ref, resid_ref, clim_ref, part_ref,
    back_ref, out_ref, sums_ref, scaled_ref, vector_ref, column_ref, class_ref, amp_ref, sems,
):
    copies = started(
        (columns_any, classes_any, amp_any), (column_ref, class_ref, amp_ref), sems
    )
    patches = ens_ref.shape[0]
    padded = vector_ref.shape[1]
    for v in range(2):
        exponent = note_above_ref[6 + v : 7 + v, :]
        vector_ref[v] = above_ref[v * padded : (v + 1) * padded, :] * jnp.exp2(
            exponent - SENT_BITS
        )
    scale(ens_above_ref, vector_ref.at[0].at, vector_ref.at[1].at, scaled_ref)
    clim = clim_ref[...] * share
    early = []
    for v, own_ref in enumerate((direction_ref, resid_ref)):
        own = own_ref[...]
        here = own * (part_ref[v] + clim * own)
        there = vector_ref[v, :patches, :] * back_ref[v, :patches, :]
        there = there * (jnp.exp2(note_ref[6 + v : 7 + v, :]) * unit)
        early.append(jnp.sum(here + there, axis=0, keepdims=True))
    for copy in copies:
        copy.wait()
    slots = (0, 1, 2)
    for start, end in blocks_of(patches):
        block = list(range(start, end))
        totals = gathered(
            scaled_ref, column_ref, class_ref, slots, corr_ref, slots, amp_ref, block
        )
        contract(ens_ref, out_ref, [inverse, inverse], block, totals)
    halves = []
    for v, own_ref in enumerate((direction_ref, resid_ref)):
        term = out_ref[v]
        halves.append(
            jnp.sum(jnp.sum(own_ref[...] * term, axis=0, keepdims=True) + early[v])
        )
        out_ref[v] = term + part_ref[v]
    place = lax.broadcasted_iota(jnp.int32, sums_ref.shape, 2)
    sums_ref[...] = jnp.where(place == 0, halves[1], halves[0])


def final_kernel(
    sums_ref, mine_ref, other_ref, clim_ref, direction_ref, resid_ref, increment_ref,
    new_ref, precond_ref,
):
    sums = jnp.sum(sums_ref[...], axis=0)
    step = sums[:, 0:1] / sums[:, 1:2]
    clim = clim_ref[...]
    first = mine_ref[0] + other_ref[0] + clim * direction_ref[...]
    new_ref[...] = increment_ref[...] + step * first
    precond_ref[...] = mine_ref[1] + other_ref[1] + clim * resid_ref[...]


def call(kernel, outs, scratch, args, specs, flops, moved):
    return pl.pallas_call(
        kernel,
        out_shape=outs,
        in_specs=specs,
        out_specs=jax.tree.map(lambda _: VMEM, outs),
        scratch_shapes=scratch,
        compiler_params=pltpu.CompilerParams(vmem_limit_bytes=24 * 1024 * 1024),
        cost_estimate=pl.CostEstimate(flops=flops, bytes_accessed=moved, transcendentals=0),
    )(*args)


def on_device(
    ens, direction, resid, increment, clim_var, corr_table, amp_table, adjacency, block_index
):
    count, patches, width = ens.shape
    groups = lax.axis_size("mem")
    tiles = lax.axis_size("tile")
    inverse = 1.0 / (count * groups - 1)
    rows = 2 * count
    up = [(i, i + 1) for i in range(tiles - 1)]
    down = [(j, i) for i, j in up]
    padded = patches + (-patches % GROUP)
    columns = adjacency.T
    classes = block_index.T

    vec = jax.ShapeDtypeStruct((2, patches, width), F32)
    flat = jax.ShapeDtypeStruct((patches, width), F32)
    local_shape = (patches, rows, width)
    product = 6 * patches * rows * width * width

    ens = jnp.transpose(ens, (1, 0, 2))
    ens_above = lax.ppermute(ens, "tile", up)
    first = call(
        first_kernel, jax.ShapeDtypeStruct((GROUP, LANES), F32), [], (), [], 4000000000, 30000000
    )
    note_shape = jax.ShapeDtypeStruct((GROUP, width), F32)
    sent_shape = (2 * padded, width)
    note = call(
        note_kernel, note_shape, [],
        (first, direction, resid, columns, classes), [VMEM] * 5,
        10 * patches * width, 400000,
    )
    note_above = lax.ppermute(note, "tile", up)
    index_above = note_above[:6, :patches].astype(jnp.int32)
    tables = [
        pltpu.SMEM(columns.shape, jnp.int32),
        pltpu.SMEM(classes.shape, jnp.int32),
        pltpu.SMEM(amp_table.shape, F32),
        pltpu.SemaphoreType.DMA((3,)),
    ]
    part, scaled, sent = call(
        functools.partial(own_kernel, inverse),
        (
            vec,
            jax.ShapeDtypeStruct(local_shape, BF16),
            jax.ShapeDtypeStruct(sent_shape, F32),
        ),
        tables,
        (columns, classes, amp_table, note, ens, direction, resid, corr_table),
        [ANY] * 3 + [VMEM] * 5,
        product, 3000000,
    )
    above = lax.ppermute(sent.astype(jnp.float16), "tile", up).astype(F32)
    unit = inverse * count * 36 * 3 * width / 2.0**SENT_BITS
    back_rows = patches + 1 + (-(patches + 1) % GROUP)
    back = call(
        functools.partial(back_kernel, unit / inverse),
        jax.ShapeDtypeStruct((2, back_rows, width), F32),
        [
            pltpu.VMEM((3,) + local_shape, F32),
            pltpu.SMEM((6, patches), jnp.int32),
            pltpu.SMEM(amp_table.shape, F32),
            pltpu.SemaphoreType.DMA((2,)),
        ],
        (index_above, amp_table, note, ens_above, scaled, corr_table),
        [ANY] * 2 + [VMEM] * 4,
        product, 3000000,
    )
    returned = lax.ppermute(back.astype(jnp.float16), "tile", down).astype(F32)
    below, sums = call(
        functools.partial(below_kernel, inverse, 1.0 / groups, unit),
        (vec, jax.ShapeDtypeStruct((tiles * groups, 1, 2), F32)),
        [pltpu.VMEM(local_shape, BF16), pltpu.VMEM((2, padded, width), F32)] + tables,
        (
            columns, classes, amp_table, ens_above, above, note_above, note, corr_table, ens,
            direction, resid, clim_var, part, back,
        ),
        [ANY] * 3 + [VMEM] * 11,
        product, 3000000,
    )
    received = returned[:, :patches] * (jnp.exp2(returned[:, patches : patches + 1]) * unit)
    mine = below + received
    if groups == 2:
        other = lax.ppermute(mine, "mem", [(0, 1), (1, 0)])
    else:
        other = lax.psum(mine, "mem")
        mine = jnp.zeros_like(mine)
    sums = lax.all_to_all(sums, ("tile", "mem"), 0, 0)
    return call(
        final_kernel, (flat, flat), [],
        (sums, mine, other, clim_var, direction, resid, increment),
        [VMEM] * 7, 20 * patches * width, 3000000,
    )


def solution(mesh):
    placed = (
        P("mem", "tile", None),
        P("tile", None),
        P("tile", None),
        P("tile", None),
        P("tile", None),
        P(),
        P(),
        P("tile", None),
        P("tile", None),
    )
    return jax.shard_map(
        on_device,
        mesh=mesh,
        in_specs=placed,
        out_specs=(P("tile", None), P("tile", None)),
        check_vma=False,
    )
```

time: 39.9 us -> 37.1 us (0.930)
  blocking collectives: 17.1 us -> 14.9 us
  starting transfers between devices: 9.88 us -> 11.8 us
  Pallas kernels: 9.73 us -> 8.73 us
  waiting for transfers between devices: 1.24 us -> 0.37 us
  local copies, waits for them, and re-layouts: 0.7 us -> 0.04 us
    ppermute x1 -> x2, starting transfers between devices: 1.29 us -> 5.75 us  [the longest x1 4.46 us: on_device(): note_above = lax.ppermute(note, 'tile', up)]
    ppermute x1, starting transfers between devices: 4.48 us -> 1.93 us  [on_device(): above = lax.ppermute(sent.astype(jnp.float16), 'tile', up).astype(F32)]
    all_to_all x1, blocking collectives: 17.1 us -> 14.9 us  [on_device(): sums = lax.all_to_all(sums, ('tile', 'mem'), 0, 0)]
    pallas_call x7 -> x6, Pallas kernels: 9.73 us -> 8.73 us  [call(): pl.pallas_call(kernel, out_shape=outs, in_specs=specs, out_specs=jax.tree...]
    ppermute x1 -> x2, waiting for transfers between devices: 1.24 us -> 0.36 us  [the longest x1 0.36 us: on_device(): returned = lax.ppermute(back.astype(jnp.float16), 'tile', down).astype(F32)]
    unnamed x20 -> x19, local copies, waits for them, and re-layouts: 0.7 us -> 0.04 us
  transfers between devices with their start and end apart: 4 -> 5, of which waited for: 1 -> 1; matrix products, arithmetic and copies ran while one was open for 0% -> 0% of each run, Pallas kernels for 21% -> 21%
where the time goes in v3:
time: 37.1 us; the launch traced here: 36.9 us
  blocking collectives  14.9 us (40%)
  starting transfers between devices  11.8 us (32%)
  Pallas kernels  8.73 us (24%)
  between operations  0.91 us (2%)
    all_to_all x1, blocking collectives, on_device(): sums = lax.all_to_all(sums, ('tile', 'mem'), 0, 0)  14.9 us
    pallas_call x6, Pallas kernels, call(): pl.pallas_call(kernel, out_shape=outs, in_specs=specs, out_specs=jax.tree...  8.73 us
    ppermute x1, starting transfers between devices, on_device(): note_above = lax.ppermute(note, 'tile', up)  4.46 us
    ppermute x1, starting transfers between devices, on_device(): ens_above = lax.ppermute(ens, 'tile', up)  2.53 us
    ppermute x1, starting transfers between devices, on_device(): above = lax.ppermute(sent.astype(jnp.float16), 'tile', up).astype(F32)  1.93 us
    ppermute x1, starting transfers between devices, on_device(): other = lax.ppermute(mine, 'mem', [(0, 1), (1, 0)])  1.59 us
    ppermute x1, starting transfers between devices, on_device(): returned = lax.ppermute(back.astype(jnp.float16), 'tile', down).astype(F32)  1.29 us
  transfers between devices with their start and end apart: 5, of which 1 were waited for; matrix products, arithmetic and copies ran while one was open for 0% of the time, Pallas kernels for 21%

profile of v3, /device:TPU:0, one launch (start us, length us, event | category | flops | bytes accessed | tf_op | source)
XLA Modules:
  0.0 36.9 jit_solution(2100493213898888175)
XLA Ops:
  0.6 0.0 copy-start
  0.6 0.0 copy-start.1
  0.7 0.0 copy-start.6
  0.7 0.0 copy-start.7
  0.7 0.0 copy-start.2
  0.7 0.0 copy-start.4
  0.7 0.0 copy-start.8
  0.7 2.5 %collective-permute-start = (bf16[150,8,256]{2,1,0:T(8,128)(2,1)}, bf16[150,8,256]{2,1,0:T(8,128)(2,1)S(1)}, u32[]{:S(2)}, u32[]{:S(2)}) collective-permute-start(bf16[150,8,256]{2,1,0:T(8,128)(2,1)} %bitcast.6), channel_id=1, source_target_pairs={{0,2},{2,4},{4,6},{6,8},{8,10},{10,12},{12,14},{14,16},{16,18},{18... | collective-permute-start | bytes 1843208 | tf_op jit(solution)/shard_map/ppermute | solution.py:258
  3.2 0.0 copy-done
  3.3 0.0 copy-done.1
  3.3 0.0 copy-done.6
  3.3 0.0 copy-done.7
  3.3 0.1 shard_map.105.note_ref
  3.4 4.5 %collective-permute-start.2 = (f32[8,256]{1,0:T(8,128)S(1)}, f32[8,256]{1,0:T(8,128)S(1)}, u32[]{:S(2)}, u32[]{:S(2)}) collective-permute-start(f32[8,256]{1,0:T(8,128)S(1)} %shard_map.105.note_ref), channel_id=1, source_target_pairs={{0,2},{2,4},{4,6},{6,8},{8,10},{10,12},{12,14},{14,16},{16,18},{18... | collective-permute-start | bytes 24584 | tf_op jit(solution)/shard_map/ppermute | solution.py:269
  7.9 0.0 copy-done.2
  7.9 0.0 copy-done.4
  7.9 0.0 copy-done.8
  7.9 2.7 %shard_map.106 = (f32[2,150,256]{2,1,0:T(8,128)S(1)}, bf16[150,16,256]{2,1,0:T(8,128)(2,1)S(1)}, f32[304,256]{1,0:T(8,128)S(1)}) custom-call(s32[9,150]{1,0:T(8,128)S(1)} %bitcast.10, s32[9,150]{1,0:T(8,128)S(1)} %bitcast.13, f32[16]{0:T(128)S(1)} %copy-done.8, f32[8,256]{1,0:T(8,128)S(1)} %shard_map.105.note_ref, bf16[150,8,256]{2,1,0:T(8,128)(2,1)S(1)} %bitcast.7, ...), custom_call_target="tpu_custom_call" | custom-call | flops 943718400 | bytes 3000000 | tf_op jit(solution)/shard_map/pallas_call | solution.py:227
  10.6 1.9 %collective-permute-start.1 = (f16[304,256]{1,0:T(8,128)(2,1)S(1)}, f16[304,256]{1,0:T(8,128)(2,1)S(1)}, u32[]{:S(2)}, u32[]{:S(2)}) collective-permute-start(f16[304,256]{1,0:T(8,128)(2,1)S(1)} %convert_element_type.15), channel_id=1, source_target_pairs={{0,2},{2,4},{4,6},{6,8},{8,10},{10,12},{12,14},{14,16},{16,18},{18... | collective-permute-start | bytes 466952 | tf_op jit(solution)/shard_map/ppermute | solution.py:289
  12.6 0.0 collective-permute-done.2.note_above_ref
  12.6 0.0 collective-permute-done.ens_ref.ens_above_ref
  12.6 0.0 copy-start.3
  12.6 2.4 %shard_map.107.back_ref = f32[2,152,256]{2,1,0:T(8,128)S(1)} custom-call(s32[6,150]{1,0:T(8,128)S(1)} %slice_convert_fusion.index_any, f32[16]{0:T(128)S(1)} %copy-done.8, f32[8,256]{1,0:T(8,128)S(1)} %shard_map.105.note_ref, bf16[150,8,256]{2,1,0:T(8,128)(2,1)S(1)} %collective-permute-done.ens_ref.ens_above_ref, ...), custom_call_target="tpu_custom_call" | custom-call | flops 943718400 | bytes 3000000 | tf_op jit(solution)/shard_map/pallas_call | solution.py:227
  15.0 1.3 %collective-permute-start.3 = (f16[2,152,256]{2,1,0:T(8,128)(2,1)S(1)}, f16[2,152,256]{2,1,0:T(8,128)(2,1)S(1)}, u32[]{:S(2)}, u32[]{:S(2)}) collective-permute-start(f16[2,152,256]{2,1,0:T(8,128)(2,1)S(1)} %convert_element_type.18), channel_id=1, source_target_pairs={{2,0},{4,2},{6,4},{8,6},{10,8},{12,10},{14,12},{16,14},{18,16},{20... | collective-permute-start | bytes 466952 | tf_op jit(solution)/shard_map/ppermute | solution.py:305
  16.3 0.0 collective-permute-done.1
  16.4 0.0 copy-done.3
  16.4 2.7 %shard_map.108 = (f32[2,150,256]{2,1,0:T(8,128)S(1)}, f32[32,1,2]{2,1,0:T(1,128)S(1)}) custom-call(s32[9,150]{1,0:T(8,128)S(1)} %bitcast.11, s32[9,150]{1,0:T(8,128)S(1)} %bitcast.14, f32[16]{0:T(128)S(1)} %copy-done.8, bf16[150,8,256]{2,1,0:T(8,128)(2,1)S(1)} %collective-permute-done.ens_ref.ens_above_ref, f32[304,256]{1,0:T(8,128)S(1)} %convert_element_type.16.above_ref, ...), custom_call_target="tpu_custom_call" | custom-call | flops 943718400 | bytes 3000000 | tf_op jit(solution)/shard_map/pallas_call | solution.py:227
  19.1 0.0 copy-start.5
  19.1 0.4 collective-permute-done.3
  19.6 1.6 %collective-permute-start.4 = (f32[2,150,256]{2,1,0:T(8,128)S(1)}, f32[2,150,256]{2,1,0:T(8,128)S(1)}, u32[]{:S(2)}, u32[]{:S(2)}) collective-permute-start(f32[2,150,256]{2,1,0:T(8,128)S(1)} %fusion.mine_ref), channel_id=1, source_target_pairs={{0,1},{1,0},{2,3},{3,2},{4,5},{5,4},{6,7},{7,6},{8,9},{9,8},{10,11... | collective-permute-start | bytes 921608 | tf_op jit(solution)/shard_map/ppermute | solution.py:320
  21.2 14.9 %all_to_all.5.sums_ref = f32[32,1,2]{2,1,0:T(1,128)S(1)} all-to-all(f32[32,1,2]{2,1,0:T(1,128)S(1)} %get-tuple-element.10), channel_id=1, replica_groups=mesh['tile'=16,'mem'=2] {'tile','mem'}, dimensions={0} | all-to-all | bytes 512 | tf_op jit(solution)/shard_map/all_to_all | solution.py:324
  36.0 0.0 collective-permute-done.4.other_ref
  36.0 0.0 copy-done.5
  36.0 0.8 %shard_map.109 = (f32[150,256]{1,0:T(8,128)}, f32[150,256]{1,0:T(8,128)}) custom-call(f32[32,1,2]{2,1,0:T(1,128)S(1)} %all_to_all.5.sums_ref, f32[2,150,256]{2,1,0:T(8,128)S(1)} %fusion.mine_ref, f32[2,150,256]{2,1,0:T(8,128)S(1)} %collective-permute-done.4.other_ref, f32[150,256]{1,0:T(8,128)S(1)} %copy-done.3, f32[150,256]{1,0:T(8,128)S(1)} %copy-done, ...), custom_call_target="tpu_custom_call" | custom-call | flops 768000 | bytes 3000000 | tf_op jit(solution)/shard_map/pallas_call | solution.py:227
  (9 shorter events, 0.1 us)
Async XLA Ops:
  0.6 2.6 %copy-start = (f32[150,256]{1,0:T(8,128)S(1)}, f32[150,256]{1,0:T(8,128)}, u32[]{:S(2)}) copy-start(f32[150,256]{1,0:T(8,128)} %direction_ref.7) | copy-start | bytes 460804
  0.6 2.6 %copy-start.1 = (f32[150,256]{1,0:T(8,128)S(1)}, f32[150,256]{1,0:T(8,128)}, u32[]{:S(2)}) copy-start(f32[150,256]{1,0:T(8,128)} %resid_ref.7) | copy-start | bytes 460804
  0.7 2.6 %copy-start.6 = (s32[150,9]{0,1:T(8,128)S(1)}, s32[150,9]{0,1:T(8,128)}, u32[]{:S(2)}) copy-start(s32[150,9]{0,1:T(8,128)} %param.16) | copy-start | bytes 16204
  0.7 2.6 %copy-start.7 = (s32[150,9]{0,1:T(8,128)S(1)}, s32[150,9]{0,1:T(8,128)}, u32[]{:S(2)}) copy-start(s32[150,9]{0,1:T(8,128)} %param.17) | copy-start | bytes 16204
  0.7 7.2 %copy-start.2 = (bf16[9,256,256]{2,1,0:T(8,128)(2,1)S(1)}, bf16[9,256,256]{2,1,0:T(8,128)(2,1)}, u32[]{:S(2)}) copy-start(bf16[9,256,256]{2,1,0:T(8,128)(2,1)} %corr_ref.5) | copy-start | bytes 3538948
  0.7 7.2 %copy-start.4 = (bf16[8,150,256]{2,0,1:T(8,128)(2,1)S(1)}, bf16[8,150,256]{2,0,1:T(8,128)(2,1)}, u32[]{:S(2)}) copy-start(bf16[8,150,256]{2,0,1:T(8,128)(2,1)} %param.9) | copy-start | bytes 1843204
  0.7 7.2 %copy-start.8 = (f32[16]{0:T(128)S(1)}, f32[16]{0:T(128)}, u32[]{:S(2)}) copy-start(f32[16]{0:T(128)} %amp_any.5) | copy-start | bytes 196
  0.7 11.9 %collective-permute-start = (bf16[150,8,256]{2,1,0:T(8,128)(2,1)}, bf16[150,8,256]{2,1,0:T(8,128)(2,1)S(1)}, u32[]{:S(2)}, u32[]{:S(2)}) collective-permute-start(bf16[150,8,256]{2,1,0:T(8,128)(2,1)} %bitcast.6), channel_id=1, source_target_pairs={{0,2},{2,4},{4,6},{6,8},{8,10},{10,12},{12,14},{14,16},{16,18},{18... | collective-permute-start | bytes 1843208 | tf_op jit(solution)/shard_map/ppermute | solution.py:258
  3.4 9.2 %collective-permute-start.2 = (f32[8,256]{1,0:T(8,128)S(1)}, f32[8,256]{1,0:T(8,128)S(1)}, u32[]{:S(2)}, u32[]{:S(2)}) collective-permute-start(f32[8,256]{1,0:T(8,128)S(1)} %shard_map.105.note_ref), channel_id=1, source_target_pairs={{0,2},{2,4},{4,6},{6,8},{8,10},{10,12},{12,14},{14,16},{16,18},{18... | collective-permute-start | bytes 24584 | tf_op jit(solution)/shard_map/ppermute | solution.py:269
  10.6 5.7 %collective-permute-start.1 = (f16[304,256]{1,0:T(8,128)(2,1)S(1)}, f16[304,256]{1,0:T(8,128)(2,1)S(1)}, u32[]{:S(2)}, u32[]{:S(2)}) collective-permute-start(f16[304,256]{1,0:T(8,128)(2,1)S(1)} %convert_element_type.15), channel_id=1, source_target_pairs={{0,2},{2,4},{4,6},{6,8},{8,10},{10,12},{12,14},{14,16},{16,18},{18... | collective-permute-start | bytes 466952 | tf_op jit(solution)/shard_map/ppermute | solution.py:289
  12.6 3.8 %copy-start.3 = (f32[150,256]{1,0:T(8,128)S(1)}, f32[150,256]{1,0:T(8,128)}, u32[]{:S(2)}) copy-start(f32[150,256]{1,0:T(8,128)} %clim_ref.3) | copy-start | bytes 460804
  15.0 4.4 %collective-permute-start.3 = (f16[2,152,256]{2,1,0:T(8,128)(2,1)S(1)}, f16[2,152,256]{2,1,0:T(8,128)(2,1)S(1)}, u32[]{:S(2)}, u32[]{:S(2)}) collective-permute-start(f16[2,152,256]{2,1,0:T(8,128)(2,1)S(1)} %convert_element_type.18), channel_id=1, source_target_pairs={{2,0},{4,2},{6,4},{8,6},{10,8},{12,10},{14,12},{16,14},{18,16},{20... | collective-permute-start | bytes 466952 | tf_op jit(solution)/shard_map/ppermute | solution.py:305
  19.1 16.9 %copy-start.5 = (f32[150,256]{1,0:T(8,128)S(1)}, f32[150,256]{1,0:T(8,128)}, u32[]{:S(2)}) copy-start(f32[150,256]{1,0:T(8,128)} %increment_ref.1) | copy-start | bytes 460804
  19.6 16.5 %collective-permute-start.4 = (f32[2,150,256]{2,1,0:T(8,128)S(1)}, f32[2,150,256]{2,1,0:T(8,128)S(1)}, u32[]{:S(2)}, u32[]{:S(2)}) collective-permute-start(f32[2,150,256]{2,1,0:T(8,128)S(1)} %fusion.mine_ref), channel_id=1, source_target_pairs={{0,1},{1,0},{2,3},{3,2},{4,5},{5,4},{6,7},{7,6},{8,9},{9,8},{10,11... | collective-permute-start | bytes 921608 | tf_op jit(solution)/shard_map/ppermute | solution.py:320

commit v4 on v3

v4 whole, which is shorter than its diff:
```python
import functools
import math

import jax
import jax.numpy as jnp
from jax import lax
from jax.experimental import pallas as pl
from jax.experimental.pallas import tpu as pltpu
from jax.sharding import PartitionSpec as P

SLOTS = 9
BLOCK = 48
GROUP = 8
LANES = 128
F32 = jnp.float32
BF16 = jnp.bfloat16
VMEM = pl.BlockSpec(memory_space=pltpu.VMEM)
SENT_BITS = 15


def blocks_of(patches):
    count = max(1, patches // BLOCK)
    starts = [i * BLOCK for i in range(count)] + [patches]
    return list(zip(starts[:-1], starts[1:]))


def scale(ens_ref, first_at, second_at, scaled_ref):
    patches = ens_ref.shape[0]

    def body(p, _):
        members = ens_ref[p].astype(F32)
        a = members * first_at[pl.ds(p, 1), :][...]
        b = members * second_at[pl.ds(p, 1), :][...]
        scaled_ref[p] = jnp.concatenate([a, b], axis=0).astype(BF16)
        return 0

    lax.fori_loop(0, patches, body, 0, unroll=10)


def gathered(scaled_ref, table_ref, corr_ref, slots, patches):
    rows = scaled_ref.shape[1]
    totals = None
    for i, slot in enumerate(slots):
        columns = [table_ref[i, p].astype(jnp.int32) for p in patches]
        left = jnp.concatenate([scaled_ref[c] for c in columns], axis=0)
        product = jnp.dot(left, corr_ref[slot], preferred_element_type=F32)
        weighted = [
            product[n * rows : (n + 1) * rows] * table_ref[3 + i, p]
            for n, p in enumerate(patches)
        ]
        totals = weighted if totals is None else [t + w for t, w in zip(totals, weighted)]
    return totals


def member_sums(terms):
    count, width = terms[0].shape
    if count != GROUP:
        return jnp.concatenate([jnp.sum(t, axis=0, keepdims=True) for t in terms], axis=0)
    used = len(terms)
    terms = terms + [jnp.zeros((count, width), F32)] * (GROUP - used)
    place = lax.broadcasted_iota(jnp.int32, (count, width), 0)
    step = 1
    while len(terms) > 1:
        keep = (place & step) == 0
        terms = [
            jnp.where(keep, a, b) + pltpu.roll(jnp.where(keep, b, a), step, 0)
            for a, b in zip(terms[::2], terms[1::2])
        ]
        step *= 2
    return terms[0][:used]


def contract(ens_ref, out_ref, factors, patches, local):
    count = ens_ref.shape[1]
    for at in range(0, len(patches), GROUP):
        group = patches[at : at + GROUP]
        members = [ens_ref[p].astype(F32) for p in group]
        for v in range(2):
            terms = [
                e * local[at + i][v * count : (v + 1) * count] for i, e in enumerate(members)
            ]
            out_ref[v, group[0] : group[0] + len(group), :] = member_sums(terms) * factors[v]


def first_kernel(out_ref):
    out_ref[...] = jnp.zeros(out_ref.shape, F32)


def table_kernel(
    first_ref, amp_ref, direction_ref, resid_ref, columns_ref, classes_ref, table_ref
):
    patches, width = direction_ref.shape
    table_ref[...] = jnp.zeros(table_ref.shape, F32)
    classes = classes_ref[...]
    weights = jnp.zeros(classes.shape, F32)
    for c in range(amp_ref.shape[1]):
        weights = jnp.where(classes == c, amp_ref[0:1, c : c + 1], weights)
    columns = columns_ref[...].astype(F32)
    for g in range(3):
        table_ref[g, 0:3, :patches] = columns[3 * g : 3 * g + 3]
        table_ref[g, 3:6, :patches] = weights[3 * g : 3 * g + 3]
    for v, vector_ref in enumerate((direction_ref, resid_ref)):
        largest = jnp.max(jnp.abs(vector_ref[...]), axis=0, keepdims=True)
        largest = jnp.maximum(jnp.max(largest, axis=1, keepdims=True), 1e-30)
        exponent = jnp.floor(jnp.log(largest) * (1.0 / math.log(2.0))) + 1.0
        for g in range(3):
            table_ref[g, 6 + v : 7 + v, :] = jnp.broadcast_to(exponent, (1, width))


def own_kernel(
    inverse, table_ref, ens_ref, direction_ref, resid_ref, corr_ref,
    part_ref, scaled_ref, sent_ref, index_ref, sem,
):
    load = pltpu.make_async_copy(table_ref.at[1], index_ref, sem)
    load.start()
    patches, width = direction_ref.shape
    padded = sent_ref.shape[0] // 2
    for v, vector_ref in enumerate((direction_ref, resid_ref)):
        at = v * padded
        factor = jnp.exp2(SENT_BITS - table_ref[1, 6 + v : 7 + v, :])
        sent_ref[at : at + patches, :] = vector_ref[...] * factor
        if padded > patches:
            sent_ref[at + patches : at + padded, :] = jnp.zeros((padded - patches, width), F32)
    scale(ens_ref, direction_ref.at, resid_ref.at, scaled_ref)
    load.wait()
    for start, end in blocks_of(patches):
        block = list(range(start, end))
        totals = gathered(scaled_ref, index_ref, corr_ref, (3, 4, 5), block)
        local = [t + scaled_ref[p].astype(F32) for t, p in zip(totals, block)]
        contract(ens_ref, part_ref, [inverse, inverse], block, local)


def back_kernel(
    unit, note_above_ref, table_ref, ens_ref, scaled_ref, corr_ref, out_ref,
    products_ref, index_ref, sem,
):
    load = pltpu.make_async_copy(note_above_ref, index_ref, sem)
    load.start()
    patches, rows, width = scaled_ref.shape
    for start, end in blocks_of(patches):
        left = scaled_ref[start:end].reshape((end - start) * rows, width)
        for i in range(3):
            product = jnp.dot(left, corr_ref[i], preferred_element_type=F32)
            products_ref[i, start:end] = product.reshape(end - start, rows, width)
    exponents = [table_ref[1, 6 + v : 7 + v, :] for v in range(2)]
    factors = [jnp.exp2(-exponent) * (1.0 / unit) for exponent in exponents]
    for v in range(2):
        out_ref[v, patches:, :] = jnp.broadcast_to(
            exponents[v], (out_ref.shape[1] - patches, width)
        )
    load.wait()
    for start, end in blocks_of(patches):
        block = list(range(start, end))
        local = [
            sum(
                products_ref[i, index_ref[i, p].astype(jnp.int32)] * index_ref[3 + i, p]
                for i in range(3)
            )
            for p in block
        ]
        contract(ens_ref, out_ref, factors, block, local)


def below_kernel(
    inverse, share, unit, table_ref, ens_above_ref, above_ref, note_above_ref,
    corr_ref, ens_ref, direction_ref, resid_ref, clim_ref, part_ref, back_ref,
    out_ref, sums_ref, scaled_ref, vector_ref, index_ref, sem,
):
    load = pltpu.make_async_copy(table_ref.at[2], index_ref, sem)
    load.start()
    patches = ens_ref.shape[0]
    padded = vector_ref.shape[1]
    for v in range(2):
        exponent = note_above_ref[6 + v : 7 + v, :]
        vector_ref[v] = above_ref[v * padded : (v + 1) * padded, :] * jnp.exp2(
            exponent - SENT_BITS
        )
    scale(ens_above_ref, vector_ref.at[0].at, vector_ref.at[1].at, scaled_ref)
    clim = clim_ref[...] * share
    early = []
    for v, own_ref in enumerate((direction_ref, resid_ref)):
        own = own_ref[...]
        here = own * (part_ref[v] + clim * own)
        there = vector_ref[v, :patches, :] * back_ref[v, :patches, :]
        there = there * (jnp.exp2(table_ref[1, 6 + v : 7 + v, :]) * unit)
        early.append(jnp.sum(here + there, axis=0, keepdims=True))
    load.wait()
    for start, end in blocks_of(patches):
        block = list(range(start, end))
        totals = gathered(scaled_ref, index_ref, corr_ref, (6, 7, 8), block)
        contract(ens_ref, out_ref, [inverse, inverse], block, totals)
    halves = []
    for v, own_ref in enumerate((direction_ref, resid_ref)):
        term = out_ref[v]
        halves.append(
            jnp.sum(jnp.sum(own_ref[...] * term, axis=0, keepdims=True) + early[v])
        )
        out_ref[v] = term + part_ref[v]
    place = lax.broadcasted_iota(jnp.int32, sums_ref.shape, 2)
    sums_ref[...] = jnp.where(place == 0, halves[1], halves[0])


def final_kernel(
    sums_ref, mine_ref, other_ref, clim_ref, direction_ref, resid_ref, increment_ref,
    new_ref, precond_ref,
):
    sums = jnp.sum(sums_ref[...], axis=0)
    step = sums[:, 0:1] / sums[:, 1:2]
    clim = clim_ref[...]
    first = mine_ref[0] + other_ref[0] + clim * direction_ref[...]
    new_ref[...] = increment_ref[...] + step * first
    precond_ref[...] = mine_ref[1] + other_ref[1] + clim * resid_ref[...]


def call(kernel, outs, scratch, args, specs, flops, moved):
    return pl.pallas_call(
        kernel,
        out_shape=outs,
        in_specs=specs,
        out_specs=jax.tree.map(lambda _: VMEM, outs),
        scratch_shapes=scratch,
        compiler_params=pltpu.CompilerParams(vmem_limit_bytes=24 * 1024 * 1024),
        cost_estimate=pl.CostEstimate(flops=flops, bytes_accessed=moved, transcendentals=0),
    )(*args)


def on_device(
    ens, direction, resid, increment, clim_var, corr_table, amp_table, adjacency, block_index
):
    count, patches, width = ens.shape
    groups = lax.axis_size("mem")
    tiles = lax.axis_size("tile")
    inverse = 1.0 / (count * groups - 1)
    rows = 2 * count
    back_way = [(i, i + 1) for i in range(tiles - 1)]
    way = [(j, i) for i, j in back_way]
    padded = patches + (-patches % GROUP)
    columns = adjacency.T
    classes = block_index.T

    vec = jax.ShapeDtypeStruct((2, patches, width), F32)
    flat = jax.ShapeDtypeStruct((patches, width), F32)
    local_shape = (patches, rows, width)
    product = 6 * patches * rows * width * width

    ens = jnp.transpose(ens, (1, 0, 2))
    ens_above = lax.ppermute(ens, "tile", way)
    first = call(
        first_kernel, jax.ShapeDtypeStruct((GROUP, LANES), F32), [], (), [], 4000000000, 30000000
    )
    sent_shape = (2 * padded, width)
    table = call(
        table_kernel,
        jax.ShapeDtypeStruct((3, GROUP, width), F32),
        [],
        (first, amp_table[None], direction, resid, columns, classes),
        [VMEM] * 6,
        10 * patches * width, 400000,
    )
    note_above = lax.ppermute(table[0], "tile", way)
    index = [pltpu.SMEM((GROUP, width), F32), pltpu.SemaphoreType.DMA]
    part, scaled, sent = call(
        functools.partial(own_kernel, inverse),
        (
            vec,
            jax.ShapeDtypeStruct(local_shape, BF16),
            jax.ShapeDtypeStruct(sent_shape, F32),
        ),
        index,
        (table, ens, direction, resid, corr_table),
        [VMEM] * 5,
        product, 3000000,
    )
    above = lax.ppermute(sent.astype(jnp.float16), "tile", way).astype(F32)
    unit = inverse * count * 36 * 3 * width / 2.0**SENT_BITS
    back_rows = patches + 1 + (-(patches + 1) % GROUP)
    back = call(
        functools.partial(back_kernel, unit / inverse),
        jax.ShapeDtypeStruct((2, back_rows, width), F32),
        [pltpu.VMEM((3,) + local_shape, F32)] + index,
        (note_above, table, ens_above, scaled, corr_table),
        [VMEM] * 5,
        product, 3000000,
    )
    returned = lax.ppermute(back.astype(jnp.float16), "tile", back_way).astype(F32)
    below, sums = call(
        functools.partial(below_kernel, inverse, 1.0 / groups, unit),
        (vec, jax.ShapeDtypeStruct((tiles * groups, 1, 2), F32)),
        [pltpu.VMEM(local_shape, BF16), pltpu.VMEM((2, padded, width), F32)] + index,
        (
            table, ens_above, above, note_above, corr_table, ens, direction, resid, clim_var,
            part, back,
        ),
        [VMEM] * 11,
        product, 3000000,
    )
    received = returned[:, :patches] * (jnp.exp2(returned[:, patches : patches + 1]) * unit)
    mine = below + received
    if groups == 2:
        other = lax.ppermute(mine, "mem", [(0, 1), (1, 0)])
    else:
        other = lax.psum(mine, "mem")
        mine = jnp.zeros_like(mine)
    sums = lax.all_to_all(sums, ("tile", "mem"), 0, 0)
    return call(
        final_kernel, (flat, flat), [],
        (sums, mine, other, clim_var, direction, resid, increment),
        [VMEM] * 7, 20 * patches * width, 3000000,
    )


def solution(mesh):
    placed = (
        P("mem", "tile", None),
        P("tile", None),
        P("tile", None),
        P("tile", None),
        P("tile", None),
        P(),
        P(),
        P("tile", None),
        P("tile", None),
    )
    return jax.shard_map(
        on_device,
        mesh=mesh,
        in_specs=placed,
        out_specs=(P("tile", None), P("tile", None)),
        check_vma=False,
    )
```

time: 37.1 us -> 36.6 us (0.987)
  starting transfers between devices: 11.8 us -> 14 us
  blocking collectives: 14.9 us -> 13.2 us
  Pallas kernels: 8.73 us -> 7.97 us
    ppermute x4, starting transfers between devices: 10.2 us -> 12.4 us  [the longest x1 8.44 us: on_device(): lax.ppermute(back.astype(jnp.float16), 'tile', back_way).astype(F32)]
    all_to_all x1, blocking collectives: 14.9 us -> 13.2 us  [on_device(): sums = lax.all_to_all(sums, ('tile', 'mem'), 0, 0)]
    pallas_call x6, Pallas kernels: 8.73 us -> 7.97 us  [call(): pl.pallas_call(kernel, out_shape=outs, in_specs=specs, out_specs=jax.tree...]
  transfers between devices with their start and end apart: 5 -> 5, of which waited for: 1 -> 0; matrix products, arithmetic and copies ran while one was open for 0% -> 0% of each run, Pallas kernels for 21% -> 20%
where the time goes in v4:
time: 36.6 us; the launch traced here: 36.4 us
  starting transfers between devices  14 us (38%)
  blocking collectives  13.2 us (36%)
  Pallas kernels  7.97 us (22%)
  between operations  0.93 us (3%)
    all_to_all x1, blocking collectives, on_device(): sums = lax.all_to_all(sums, ('tile', 'mem'), 0, 0)  13.2 us
    ppermute x1, starting transfers between devices, on_device(): lax.ppermute(back.astype(jnp.float16), 'tile', back_way).astype(F32)  8.44 us
    pallas_call x6, Pallas kernels, call(): pl.pallas_call(kernel, out_shape=outs, in_specs=specs, out_specs=jax.tree...  7.97 us
    ppermute x1, starting transfers between devices, on_device(): other = lax.ppermute(mine, 'mem', [(0, 1), (1, 0)])  1.59 us
    ppermute x1, starting transfers between devices, on_device(): ens_above = lax.ppermute(ens, 'tile', way)  1.42 us
    ppermute x1, starting transfers between devices, on_device(): note_above = lax.ppermute(table[0], 'tile', way)  1.29 us
    ppermute x1, starting transfers between devices, on_device(): above = lax.ppermute(sent.astype(jnp.float16), 'tile', way).astype(F32)  1.29 us
  transfers between devices with their start and end apart: 5, of which 0 were waited for; matrix products, arithmetic and copies ran while one was open for 0% of the time, Pallas kernels for 20%

profile of v4, /device:TPU:0, one launch (start us, length us, event | category | flops | bytes accessed | tf_op | source)
XLA Modules:
  0.0 36.4 jit_solution(4870369788669552793)
XLA Ops:
  0.6 0.0 copy-start
  0.6 0.0 copy-start.1
  0.7 0.0 copy-start.6
  0.7 0.0 copy-start.7
  0.7 0.0 copy-start.8
  0.7 0.0 copy-start.2
  0.7 0.0 copy-start.4
  0.7 1.4 %collective-permute-start = (bf16[150,8,256]{2,1,0:T(8,128)(2,1)}, bf16[150,8,256]{2,1,0:T(8,128)(2,1)S(1)}, u32[]{:S(2)}, u32[]{:S(2)}) collective-permute-start(bf16[150,8,256]{2,1,0:T(8,128)(2,1)} %bitcast.9), channel_id=1, source_target_pairs={{2,0},{4,2},{6,4},{8,6},{10,8},{12,10},{14,12},{16,14},{18,16},{20... | collective-permute-start | bytes 1843208 | tf_op jit(solution)/shard_map/ppermute | solution.py:247
  2.1 0.0 copy-done
  2.2 0.0 copy-done.1
  2.2 0.0 copy-done.6
  2.2 0.0 copy-done.7
  2.2 0.0 copy-done.8
  2.2 0.1 shard_map.105.table_ref
  2.3 1.3 %collective-permute-start.2 = (f32[8,256]{1,0:T(8,128)S(1)}, f32[8,256]{1,0:T(8,128)S(1)}, u32[]{:S(2)}, u32[]{:S(2)}) collective-permute-start(f32[8,256]{1,0:T(8,128)S(1)} %slice_bitcast_fusion), channel_id=1, source_target_pairs={{2,0},{4,2},{6,4},{8,6},{10,8},{12,10},{14,12},{16,14},{18,16},{20... | collective-permute-start | bytes 24584 | tf_op jit(solution)/shard_map/ppermute | solution.py:260
  3.6 0.0 copy-done.2
  3.6 0.0 copy-done.4
  3.7 2.4 %shard_map.106 = (f32[2,150,256]{2,1,0:T(8,128)S(1)}, bf16[150,16,256]{2,1,0:T(8,128)(2,1)S(1)}, f32[304,256]{1,0:T(8,128)S(1)}) custom-call(f32[3,8,256]{2,1,0:T(8,128)S(1)} %shard_map.105.table_ref, bf16[150,8,256]{2,1,0:T(8,128)(2,1)S(1)} %bitcast.10, f32[150,256]{1,0:T(8,128)S(1)} %copy-done, f32[150,256]{1,0:T(8,128)S(1)} %copy-done.1, ...), custom_call_target="tpu_custom_call" | custom-call | flops 943718400 | bytes 3000000 | tf_op jit(solution)/shard_map/pallas_call | solution.py:216
  6.1 1.3 %collective-permute-start.1 = (f16[304,256]{1,0:T(8,128)(2,1)S(1)}, f16[304,256]{1,0:T(8,128)(2,1)S(1)}, u32[]{:S(2)}, u32[]{:S(2)}) collective-permute-start(f16[304,256]{1,0:T(8,128)(2,1)S(1)} %convert_element_type.12), channel_id=1, source_target_pairs={{2,0},{4,2},{6,4},{8,6},{10,8},{12,10},{14,12},{16,14},{18,16},{20... | collective-permute-start | bytes 466952 | tf_op jit(solution)/shard_map/ppermute | solution.py:274
  7.4 0.0 collective-permute-done.2.note_above_ref
  7.4 0.0 collective-permute-done.ens_ref.ens_above_ref
  7.4 0.0 copy-start.3
  7.4 2.3 %shard_map.107.back_ref = f32[2,152,256]{2,1,0:T(8,128)S(1)} custom-call(f32[8,256]{1,0:T(8,128)S(1)} %collective-permute-done.2.note_above_ref, f32[3,8,256]{2,1,0:T(8,128)S(1)} %shard_map.105.table_ref, bf16[150,8,256]{2,1,0:T(8,128)(2,1)S(1)} %collective-permute-done.ens_ref.ens_above_ref, bf16[150,16,256]{2,1,0:T(8,128)(2,1)S(1)} %get-tuple-element.9.scaled_ref, ...), custom_call_target="tpu_custom_call" | custom-call | flops 943718400 | bytes 3000000 | tf_op jit(solution)/shard_map/pallas_call | solution.py:216
  9.7 8.4 %collective-permute-start.3 = (f16[2,152,256]{2,1,0:T(8,128)(2,1)S(1)}, f16[2,152,256]{2,1,0:T(8,128)(2,1)S(1)}, u32[]{:S(2)}, u32[]{:S(2)}) collective-permute-start(f16[2,152,256]{2,1,0:T(8,128)(2,1)S(1)} %convert_element_type.14), channel_id=1, source_target_pairs={{0,2},{2,4},{4,6},{6,8},{8,10},{10,12},{12,14},{14,16},{16,18},{18... | collective-permute-start | bytes 466952 | tf_op jit(solution)/shard_map/ppermute | solution.py:285
  18.1 0.0 collective-permute-done.1
  18.2 0.0 copy-done.3
  18.2 2.4 %shard_map.108 = (f32[2,150,256]{2,1,0:T(8,128)S(1)}, f32[32,1,2]{2,1,0:T(1,128)S(1)}) custom-call(f32[3,8,256]{2,1,0:T(8,128)S(1)} %shard_map.105.table_ref, bf16[150,8,256]{2,1,0:T(8,128)(2,1)S(1)} %collective-permute-done.ens_ref.ens_above_ref, f32[304,256]{1,0:T(8,128)S(1)} %convert_element_type.13.above_ref, ...), custom_call_target="tpu_custom_call" | custom-call | flops 943718400 | bytes 3000000 | tf_op jit(solution)/shard_map/pallas_call | solution.py:216
  20.6 0.0 copy-start.5
  20.6 0.0 collective-permute-done.3
  20.7 1.6 %collective-permute-start.4 = (f32[2,150,256]{2,1,0:T(8,128)S(1)}, f32[2,150,256]{2,1,0:T(8,128)S(1)}, u32[]{:S(2)}, u32[]{:S(2)}) collective-permute-start(f32[2,150,256]{2,1,0:T(8,128)S(1)} %fusion.mine_ref), channel_id=1, source_target_pairs={{0,1},{1,0},{2,3},{3,2},{4,5},{5,4},{6,7},{7,6},{8,9},{9,8},{10,11... | collective-permute-start | bytes 921608 | tf_op jit(solution)/shard_map/ppermute | solution.py:300
  22.3 13.2 %all_to_all.5.sums_ref = f32[32,1,2]{2,1,0:T(1,128)S(1)} all-to-all(f32[32,1,2]{2,1,0:T(1,128)S(1)} %get-tuple-element.10), channel_id=1, replica_groups=mesh['tile'=16,'mem'=2] {'tile','mem'}, dimensions={0} | all-to-all | bytes 512 | tf_op jit(solution)/shard_map/all_to_all | solution.py:304
  35.5 0.0 collective-permute-done.4.other_ref
  35.5 0.0 copy-done.5
  35.5 0.8 %shard_map.109 = (f32[150,256]{1,0:T(8,128)}, f32[150,256]{1,0:T(8,128)}) custom-call(f32[32,1,2]{2,1,0:T(1,128)S(1)} %all_to_all.5.sums_ref, f32[2,150,256]{2,1,0:T(8,128)S(1)} %fusion.mine_ref, f32[2,150,256]{2,1,0:T(8,128)S(1)} %collective-permute-done.4.other_ref, f32[150,256]{1,0:T(8,128)S(1)} %copy-done.3, f32[150,256]{1,0:T(8,128)S(1)} %copy-done, ...), custom_call_target="tpu_custom_call" | custom-call | flops 768000 | bytes 3000000 | tf_op jit(solution)/shard_map/pallas_call | solution.py:216
  (9 shorter events, 0.1 us)
Async XLA Ops:
  0.6 1.5 %copy-start = (f32[150,256]{1,0:T(8,128)S(1)}, f32[150,256]{1,0:T(8,128)}, u32[]{:S(2)}) copy-start(f32[150,256]{1,0:T(8,128)} %direction_ref.7) | copy-start | bytes 460804
  0.6 1.5 %copy-start.1 = (f32[150,256]{1,0:T(8,128)S(1)}, f32[150,256]{1,0:T(8,128)}, u32[]{:S(2)}) copy-start(f32[150,256]{1,0:T(8,128)} %resid_ref.7) | copy-start | bytes 460804
  0.7 1.5 %copy-start.6 = (s32[150,9]{0,1:T(8,128)S(1)}, s32[150,9]{0,1:T(8,128)}, u32[]{:S(2)}) copy-start(s32[150,9]{0,1:T(8,128)} %param.16) | copy-start | bytes 16204
  0.7 1.5 %copy-start.7 = (s32[150,9]{0,1:T(8,128)S(1)}, s32[150,9]{0,1:T(8,128)}, u32[]{:S(2)}) copy-start(s32[150,9]{0,1:T(8,128)} %param.17) | copy-start | bytes 16204
  0.7 1.5 %copy-start.8 = (f32[16]{0:T(128)S(1)}, f32[16]{0:T(128)}, u32[]{:S(2)}) copy-start(f32[16]{0:T(128)} %param.15) | copy-start | bytes 196
  0.7 3.0 %copy-start.2 = (bf16[9,256,256]{2,1,0:T(8,128)(2,1)S(1)}, bf16[9,256,256]{2,1,0:T(8,128)(2,1)}, u32[]{:S(2)}) copy-start(bf16[9,256,256]{2,1,0:T(8,128)(2,1)} %corr_ref.5) | copy-start | bytes 3538948
  0.7 3.0 %copy-start.4 = (bf16[8,150,256]{2,0,1:T(8,128)(2,1)S(1)}, bf16[8,150,256]{2,0,1:T(8,128)(2,1)}, u32[]{:S(2)}) copy-start(bf16[8,150,256]{2,0,1:T(8,128)(2,1)} %param.9) | copy-start | bytes 1843204
  0.7 6.7 %collective-permute-start = (bf16[150,8,256]{2,1,0:T(8,128)(2,1)}, bf16[150,8,256]{2,1,0:T(8,128)(2,1)S(1)}, u32[]{:S(2)}, u32[]{:S(2)}) collective-permute-start(bf16[150,8,256]{2,1,0:T(8,128)(2,1)} %bitcast.9), channel_id=1, source_target_pairs={{2,0},{4,2},{6,4},{8,6},{10,8},{12,10},{14,12},{16,14},{18,16},{20... | collective-permute-start | bytes 1843208 | tf_op jit(solution)/shard_map/ppermute | solution.py:247
  2.3 5.0 %collective-permute-start.2 = (f32[8,256]{1,0:T(8,128)S(1)}, f32[8,256]{1,0:T(8,128)S(1)}, u32[]{:S(2)}, u32[]{:S(2)}) collective-permute-start(f32[8,256]{1,0:T(8,128)S(1)} %slice_bitcast_fusion), channel_id=1, source_target_pairs={{2,0},{4,2},{6,4},{8,6},{10,8},{12,10},{14,12},{16,14},{18,16},{20... | collective-permute-start | bytes 24584 | tf_op jit(solution)/shard_map/ppermute | solution.py:260
  6.1 12.1 %collective-permute-start.1 = (f16[304,256]{1,0:T(8,128)(2,1)S(1)}, f16[304,256]{1,0:T(8,128)(2,1)S(1)}, u32[]{:S(2)}, u32[]{:S(2)}) collective-permute-start(f16[304,256]{1,0:T(8,128)(2,1)S(1)} %convert_element_type.12), channel_id=1, source_target_pairs={{2,0},{4,2},{6,4},{8,6},{10,8},{12,10},{14,12},{16,14},{18,16},{20... | collective-permute-start | bytes 466952 | tf_op jit(solution)/shard_map/ppermute | solution.py:274
  7.4 10.8 %copy-start.3 = (f32[150,256]{1,0:T(8,128)S(1)}, f32[150,256]{1,0:T(8,128)}, u32[]{:S(2)}) copy-start(f32[150,256]{1,0:T(8,128)} %clim_ref.3) | copy-start | bytes 460804
  9.7 10.9 %collective-permute-start.3 = (f16[2,152,256]{2,1,0:T(8,128)(2,1)S(1)}, f16[2,152,256]{2,1,0:T(8,128)(2,1)S(1)}, u32[]{:S(2)}, u32[]{:S(2)}) collective-permute-start(f16[2,152,256]{2,1,0:T(8,128)(2,1)S(1)} %convert_element_type.14), channel_id=1, source_target_pairs={{0,2},{2,4},{4,6},{6,8},{8,10},{10,12},{12,14},{14,16},{16,18},{18... | collective-permute-start | bytes 466952 | tf_op jit(solution)/shard_map/ppermute | solution.py:285
  20.6 15.0 %copy-start.5 = (f32[150,256]{1,0:T(8,128)S(1)}, f32[150,256]{1,0:T(8,128)}, u32[]{:S(2)}) copy-start(f32[150,256]{1,0:T(8,128)} %increment_ref.1) | copy-start | bytes 460804
  20.7 14.8 %collective-permute-start.4 = (f32[2,150,256]{2,1,0:T(8,128)S(1)}, f32[2,150,256]{2,1,0:T(8,128)S(1)}, u32[]{:S(2)}, u32[]{:S(2)}) collective-permute-start(f32[2,150,256]{2,1,0:T(8,128)S(1)} %fusion.mine_ref), channel_id=1, source_target_pairs={{0,1},{1,0},{2,3},{3,2},{4,5},{5,4},{6,7},{7,6},{8,9},{9,8},{10,11... | collective-permute-start | bytes 921608 | tf_op jit(solution)/shard_map/ppermute | solution.py:300

commit v5 on v4

--- a/solution.py
+++ b/solution.py
@@ -130,18 +130,21 @@
         contract(ens_ref, part_ref, [inverse, inverse], block, local)
 
 
-def back_kernel(
-    unit, note_above_ref, table_ref, ens_ref, scaled_ref, corr_ref, out_ref,
-    products_ref, index_ref, sem,
-):
-    load = pltpu.make_async_copy(note_above_ref, index_ref, sem)
-    load.start()
+def products_kernel(scaled_ref, corr_ref, products_ref):
     patches, rows, width = scaled_ref.shape
     for start, end in blocks_of(patches):
         left = scaled_ref[start:end].reshape((end - start) * rows, width)
         for i in range(3):
             product = jnp.dot(left, corr_ref[i], preferred_element_type=F32)
             products_ref[i, start:end] = product.reshape(end - start, rows, width)
+
+
+def back_kernel(
+    unit, note_above_ref, table_ref, ens_ref, products_ref, out_ref, index_ref, sem,
+):
+    load = pltpu.make_async_copy(note_above_ref, index_ref, sem)
+    load.start()
+    patches, _, width = ens_ref.shape
     exponents = [table_ref[1, 6 + v : 7 + v, :] for v in range(2)]
     factors = [jnp.exp2(-exponent) * (1.0 / unit) for exponent in exponents]
     for v in range(2):
@@ -271,15 +274,24 @@
         [VMEM] * 5,
         product, 3000000,
     )
-    above = lax.ppermute(sent.astype(jnp.float16), "tile", way).astype(F32)
+    sent16 = sent.astype(jnp.float16)
+    above = lax.ppermute(sent16, "tile", way).astype(F32)
     unit = inverse * count * 36 * 3 * width / 2.0**SENT_BITS
     back_rows = patches + 1 + (-(patches + 1) % GROUP)
+    products = call(
+        products_kernel,
+        jax.ShapeDtypeStruct((3,) + local_shape, F32),
+        [],
+        (scaled, corr_table),
+        [VMEM] * 2,
+        product, 3000000,
+    )
     back = call(
         functools.partial(back_kernel, unit / inverse),
         jax.ShapeDtypeStruct((2, back_rows, width), F32),
-        [pltpu.VMEM((3,) + local_shape, F32)] + index,
-        (note_above, table, ens_above, scaled, corr_table),
-        [VMEM] * 5,
+        index,
+        (note_above, table, ens_above, products),
+        [VMEM] * 4,
         product, 3000000,
     )
     returned = lax.ppermute(back.astype(jnp.float16), "tile", back_way).astype(F32)

time: 36.6 us -> 36.3 us (level)
  starting transfers between devices: 14 us -> 12.9 us
  Pallas kernels: 7.97 us -> 8.6 us
    ppermute x1, starting transfers between devices: 8.44 us -> 7.34 us  [on_device(): lax.ppermute(back.astype(jnp.float16), 'tile', back_way).astype(F32)]
    pallas_call x6 -> x7, Pallas kernels: 7.97 us -> 8.6 us  [call(): pl.pallas_call(kernel, out_shape=outs, in_specs=specs, out_specs=jax.tree...]
  transfers between devices with their start and end apart: 5 -> 5, of which waited for: 0 -> 0; matrix products, arithmetic and copies ran while one was open for 0% -> 0% of each run, Pallas kernels for 20% -> 22%
where the time goes in v5:
time: 36.3 us; the launch traced here: 36.1 us
  blocking collectives  13.4 us (37%)
  starting transfers between devices  12.9 us (36%)
  Pallas kernels  8.6 us (24%)
  between operations  0.94 us (3%)
    all_to_all x1, blocking collectives, on_device(): sums = lax.all_to_all(sums, ('tile', 'mem'), 0, 0)  13.4 us
    pallas_call x7, Pallas kernels, call(): pl.pallas_call(kernel, out_shape=outs, in_specs=specs, out_specs=jax.tree...  8.6 us
    ppermute x1, starting transfers between devices, on_device(): lax.ppermute(back.astype(jnp.float16), 'tile', back_way).astype(F32)  7.34 us
    ppermute x1, starting transfers between devices, on_device(): other = lax.ppermute(mine, 'mem', [(0, 1), (1, 0)])  1.59 us
    ppermute x1, starting transfers between devices, on_device(): ens_above = lax.ppermute(ens, 'tile', way)  1.42 us
    ppermute x1, starting transfers between devices, on_device(): note_above = lax.ppermute(table[0], 'tile', way)  1.29 us
    ppermute x1, starting transfers between devices, on_device(): above = lax.ppermute(sent16, 'tile', way).astype(F32)  1.29 us
  transfers between devices with their start and end apart: 5, of which 0 were waited for; matrix products, arithmetic and copies ran while one was open for 0% of the time, Pallas kernels for 22%

profile of v5, /device:TPU:0, one launch (start us, length us, event | category | flops | bytes accessed | tf_op | source)
XLA Modules:
  0.0 36.1 jit_solution(9887424256412650448)
XLA Ops:
  0.6 0.0 copy-start.1
  0.6 0.0 copy-start.2
  0.7 0.0 copy-start.6
  0.7 0.0 copy-start.7
  0.7 0.0 copy-start.8
  0.7 0.0 copy-start
  0.7 0.0 copy-start.4
  0.7 1.4 %collective-permute-start = (bf16[150,8,256]{2,1,0:T(8,128)(2,1)}, bf16[150,8,256]{2,1,0:T(8,128)(2,1)S(1)}, u32[]{:S(2)}, u32[]{:S(2)}) collective-permute-start(bf16[150,8,256]{2,1,0:T(8,128)(2,1)} %bitcast.9), channel_id=1, source_target_pairs={{2,0},{4,2},{6,4},{8,6},{10,8},{12,10},{14,12},{16,14},{18,16},{20... | collective-permute-start | bytes 1843208 | tf_op jit(solution)/shard_map/ppermute | solution.py:250
  2.1 0.0 copy-done.1
  2.2 0.0 copy-done.2
  2.2 0.0 copy-done.6
  2.2 0.0 copy-done.7
  2.2 0.0 copy-done.8
  2.2 0.1 shard_map.105.table_ref
  2.3 1.3 %collective-permute-start.2 = (f32[8,256]{1,0:T(8,128)S(1)}, f32[8,256]{1,0:T(8,128)S(1)}, u32[]{:S(2)}, u32[]{:S(2)}) collective-permute-start(f32[8,256]{1,0:T(8,128)S(1)} %slice_bitcast_fusion), channel_id=1, source_target_pairs={{2,0},{4,2},{6,4},{8,6},{10,8},{12,10},{14,12},{16,14},{18,16},{20... | collective-permute-start | bytes 24584 | tf_op jit(solution)/shard_map/ppermute | solution.py:263
  3.6 0.0 copy-done
  3.6 0.0 copy-done.4
  3.7 2.3 %shard_map.106 = (f32[2,150,256]{2,1,0:T(8,128)S(1)}, bf16[150,16,256]{2,1,0:T(8,128)(2,1)S(1)}, f32[304,256]{1,0:T(8,128)S(1)}) custom-call(f32[3,8,256]{2,1,0:T(8,128)S(1)} %shard_map.105.table_ref, bf16[150,8,256]{2,1,0:T(8,128)(2,1)S(1)} %bitcast.10, f32[150,256]{1,0:T(8,128)S(1)} %copy-done.1, f32[150,256]{1,0:T(8,128)S(1)} %copy-done.2, ...), custom_call_target="tpu_custom_call" | custom-call | flops 943718400 | bytes 3000000 | tf_op jit(solution)/shard_map/pallas_call | solution.py:219
  6.0 1.3 %collective-permute-start.1 = (f16[304,256]{1,0:T(8,128)(2,1)S(1)}, f16[304,256]{1,0:T(8,128)(2,1)S(1)}, u32[]{:S(2)}, u32[]{:S(2)}) collective-permute-start(f16[304,256]{1,0:T(8,128)(2,1)S(1)} %convert_element_type.12), channel_id=1, source_target_pairs={{2,0},{4,2},{6,4},{8,6},{10,8},{12,10},{14,12},{16,14},{18,16},{20... | collective-permute-start | bytes 466952 | tf_op jit(solution)/shard_map/ppermute | solution.py:278
  7.3 1.1 %shard_map.107.products_ref = f32[3,150,16,256]{3,2,1,0:T(8,128)S(1)} custom-call(bf16[150,16,256]{2,1,0:T(8,128)(2,1)S(1)} %get-tuple-element.9.scaled_ref, bf16[9,256,256]{2,1,0:T(8,128)(2,1)S(1)} %copy-done), custom_call_target="tpu_custom_call" | custom-call | flops 943718400 | bytes 3000000 | tf_op jit(solution)/shard_map/pallas_call | solution.py:219
  8.5 0.0 copy-start.3
  8.5 0.0 collective-permute-done.2.note_above_ref
  8.5 0.0 collective-permute-done.ens_ref.ens_above_ref
  8.5 1.8 %shard_map.108.back_ref = f32[2,152,256]{2,1,0:T(8,128)S(1)} custom-call(f32[8,256]{1,0:T(8,128)S(1)} %collective-permute-done.2.note_above_ref, f32[3,8,256]{2,1,0:T(8,128)S(1)} %shard_map.105.table_ref, bf16[150,8,256]{2,1,0:T(8,128)(2,1)S(1)} %collective-permute-done.ens_ref.ens_above_ref, f32[3,150,16,256]{3,2,1,0:T(8,128)S(1)} %shard_map.107.products_ref), custom_call_target="tpu_custom_call" | custom-call | flops 943718400 | bytes 3000000 | tf_op jit(solution)/shard_map/pallas_call | solution.py:219
  10.3 7.3 %collective-permute-start.3 = (f16[2,152,256]{2,1,0:T(8,128)(2,1)S(1)}, f16[2,152,256]{2,1,0:T(8,128)(2,1)S(1)}, u32[]{:S(2)}, u32[]{:S(2)}) collective-permute-start(f16[2,152,256]{2,1,0:T(8,128)(2,1)S(1)} %convert_element_type.14), channel_id=1, source_target_pairs={{0,2},{2,4},{4,6},{6,8},{8,10},{10,12},{12,14},{14,16},{16,18},{18... | collective-permute-start | bytes 466952 | tf_op jit(solution)/shard_map/ppermute | solution.py:297
  17.7 0.0 collective-permute-done.1
  17.7 0.0 copy-done.3
  17.7 2.4 %shard_map.109 = (f32[2,150,256]{2,1,0:T(8,128)S(1)}, f32[32,1,2]{2,1,0:T(1,128)S(1)}) custom-call(f32[3,8,256]{2,1,0:T(8,128)S(1)} %shard_map.105.table_ref, bf16[150,8,256]{2,1,0:T(8,128)(2,1)S(1)} %collective-permute-done.ens_ref.ens_above_ref, f32[304,256]{1,0:T(8,128)S(1)} %convert_element_type.13.above_ref, ...), custom_call_target="tpu_custom_call" | custom-call | flops 943718400 | bytes 3000000 | tf_op jit(solution)/shard_map/pallas_call | solution.py:219
  20.1 0.0 copy-start.5
  20.1 0.0 collective-permute-done.3
  20.2 1.6 %collective-permute-start.4 = (f32[2,150,256]{2,1,0:T(8,128)S(1)}, f32[2,150,256]{2,1,0:T(8,128)S(1)}, u32[]{:S(2)}, u32[]{:S(2)}) collective-permute-start(f32[2,150,256]{2,1,0:T(8,128)S(1)} %fusion.mine_ref), channel_id=1, source_target_pairs={{0,1},{1,0},{2,3},{3,2},{4,5},{5,4},{6,7},{7,6},{8,9},{9,8},{10,11... | collective-permute-start | bytes 921608 | tf_op jit(solution)/shard_map/ppermute | solution.py:312
  21.8 13.4 %all_to_all.5.sums_ref = f32[32,1,2]{2,1,0:T(1,128)S(1)} all-to-all(f32[32,1,2]{2,1,0:T(1,128)S(1)} %get-tuple-element.10), channel_id=1, replica_groups=mesh['tile'=16,'mem'=2] {'tile','mem'}, dimensions={0} | all-to-all | bytes 512 | tf_op jit(solution)/shard_map/all_to_all | solution.py:316
  35.2 0.0 collective-permute-done.4.other_ref
  35.2 0.0 copy-done.5
  35.2 0.8 %shard_map.110 = (f32[150,256]{1,0:T(8,128)}, f32[150,256]{1,0:T(8,128)}) custom-call(f32[32,1,2]{2,1,0:T(1,128)S(1)} %all_to_all.5.sums_ref, f32[2,150,256]{2,1,0:T(8,128)S(1)} %fusion.mine_ref, f32[2,150,256]{2,1,0:T(8,128)S(1)} %collective-permute-done.4.other_ref, f32[150,256]{1,0:T(8,128)S(1)} %copy-done.3, f32[150,256]{1,0:T(8,128)S(1)} %copy-done.1, ...), custom_call_target="tpu_custom_call" | custom-call | flops 768000 | bytes 3000000 | tf_op jit(solution)/shard_map/pallas_call | solution.py:219
  (9 shorter events, 0.1 us)
Async XLA Ops:
  0.6 1.5 %copy-start.1 = (f32[150,256]{1,0:T(8,128)S(1)}, f32[150,256]{1,0:T(8,128)}, u32[]{:S(2)}) copy-start(f32[150,256]{1,0:T(8,128)} %direction_ref.7) | copy-start | bytes 460804
  0.6 1.5 %copy-start.2 = (f32[150,256]{1,0:T(8,128)S(1)}, f32[150,256]{1,0:T(8,128)}, u32[]{:S(2)}) copy-start(f32[150,256]{1,0:T(8,128)} %resid_ref.7) | copy-start | bytes 460804
  0.7 1.5 %copy-start.6 = (s32[150,9]{0,1:T(8,128)S(1)}, s32[150,9]{0,1:T(8,128)}, u32[]{:S(2)}) copy-start(s32[150,9]{0,1:T(8,128)} %param.16) | copy-start | bytes 16204
  0.7 1.5 %copy-start.7 = (s32[150,9]{0,1:T(8,128)S(1)}, s32[150,9]{0,1:T(8,128)}, u32[]{:S(2)}) copy-start(s32[150,9]{0,1:T(8,128)} %param.17) | copy-start | bytes 16204
  0.7 1.5 %copy-start.8 = (f32[16]{0:T(128)S(1)}, f32[16]{0:T(128)}, u32[]{:S(2)}) copy-start(f32[16]{0:T(128)} %param.15) | copy-start | bytes 196
  0.7 3.0 %copy-start = (bf16[9,256,256]{2,1,0:T(8,128)(2,1)S(1)}, bf16[9,256,256]{2,1,0:T(8,128)(2,1)}, u32[]{:S(2)}) copy-start(bf16[9,256,256]{2,1,0:T(8,128)(2,1)} %corr_ref.5) | copy-start | bytes 3538948
  0.7 3.0 %copy-start.4 = (bf16[8,150,256]{2,0,1:T(8,128)(2,1)S(1)}, bf16[8,150,256]{2,0,1:T(8,128)(2,1)}, u32[]{:S(2)}) copy-start(bf16[8,150,256]{2,0,1:T(8,128)(2,1)} %param.9) | copy-start | bytes 1843204
  0.7 7.8 %collective-permute-start = (bf16[150,8,256]{2,1,0:T(8,128)(2,1)}, bf16[150,8,256]{2,1,0:T(8,128)(2,1)S(1)}, u32[]{:S(2)}, u32[]{:S(2)}) collective-permute-start(bf16[150,8,256]{2,1,0:T(8,128)(2,1)} %bitcast.9), channel_id=1, source_target_pairs={{2,0},{4,2},{6,4},{8,6},{10,8},{12,10},{14,12},{16,14},{18,16},{20... | collective-permute-start | bytes 1843208 | tf_op jit(solution)/shard_map/ppermute | solution.py:250
  2.3 6.1 %collective-permute-start.2 = (f32[8,256]{1,0:T(8,128)S(1)}, f32[8,256]{1,0:T(8,128)S(1)}, u32[]{:S(2)}, u32[]{:S(2)}) collective-permute-start(f32[8,256]{1,0:T(8,128)S(1)} %slice_bitcast_fusion), channel_id=1, source_target_pairs={{2,0},{4,2},{6,4},{8,6},{10,8},{12,10},{14,12},{16,14},{18,16},{20... | collective-permute-start | bytes 24584 | tf_op jit(solution)/shard_map/ppermute | solution.py:263
  6.0 11.7 %collective-permute-start.1 = (f16[304,256]{1,0:T(8,128)(2,1)S(1)}, f16[304,256]{1,0:T(8,128)(2,1)S(1)}, u32[]{:S(2)}, u32[]{:S(2)}) collective-permute-start(f16[304,256]{1,0:T(8,128)(2,1)S(1)} %convert_element_type.12), channel_id=1, source_target_pairs={{2,0},{4,2},{6,4},{8,6},{10,8},{12,10},{14,12},{16,14},{18,16},{20... | collective-permute-start | bytes 466952 | tf_op jit(solution)/shard_map/ppermute | solution.py:278
  8.5 9.3 %copy-start.3 = (f32[150,256]{1,0:T(8,128)S(1)}, f32[150,256]{1,0:T(8,128)}, u32[]{:S(2)}) copy-start(f32[150,256]{1,0:T(8,128)} %clim_ref.3) | copy-start | bytes 460804
  10.3 9.8 %collective-permute-start.3 = (f16[2,152,256]{2,1,0:T(8,128)(2,1)S(1)}, f16[2,152,256]{2,1,0:T(8,128)(2,1)S(1)}, u32[]{:S(2)}, u32[]{:S(2)}) collective-permute-start(f16[2,152,256]{2,1,0:T(8,128)(2,1)S(1)} %convert_element_type.14), channel_id=1, source_target_pairs={{0,2},{2,4},{4,6},{6,8},{8,10},{10,12},{12,14},{14,16},{16,18},{18... | collective-permute-start | bytes 466952 | tf_op jit(solution)/shard_map/ppermute | solution.py:297
  20.1 15.1 %copy-start.5 = (f32[150,256]{1,0:T(8,128)S(1)}, f32[150,256]{1,0:T(8,128)}, u32[]{:S(2)}) copy-start(f32[150,256]{1,0:T(8,128)} %increment_ref.1) | copy-start | bytes 460804
  20.2 15.0 %collective-permute-start.4 = (f32[2,150,256]{2,1,0:T(8,128)S(1)}, f32[2,150,256]{2,1,0:T(8,128)S(1)}, u32[]{:S(2)}, u32[]{:S(2)}) collective-permute-start(f32[2,150,256]{2,1,0:T(8,128)S(1)} %fusion.mine_ref), channel_id=1, source_target_pairs={{0,1},{1,0},{2,3},{3,2},{4,5},{5,4},{6,7},{7,6},{8,9},{9,8},{10,11... | collective-permute-start | bytes 921608 | tf_op jit(solution)/shard_map/ppermute | solution.py:312

commit v6 on v5

--- a/solution.py
+++ b/solution.py
@@ -87,7 +87,8 @@
 
 
 def table_kernel(
-    first_ref, amp_ref, direction_ref, resid_ref, columns_ref, classes_ref, table_ref
+    first_ref, amp_ref, direction_ref, resid_ref, columns_ref, classes_ref, table_ref,
+    sent_ref,
 ):
     patches, width = direction_ref.shape
     table_ref[...] = jnp.zeros(table_ref.shape, F32)
@@ -105,15 +106,6 @@
         exponent = jnp.floor(jnp.log(largest) * (1.0 / math.log(2.0))) + 1.0
         for g in range(3):
             table_ref[g, 6 + v : 7 + v, :] = jnp.broadcast_to(exponent, (1, width))
-
-
-def own_kernel(
-    inverse, table_ref, ens_ref, direction_ref, resid_ref, corr_ref,
-    part_ref, scaled_ref, sent_ref, index_ref, sem,
-):
-    load = pltpu.make_async_copy(table_ref.at[1], index_ref, sem)
-    load.start()
-    patches, width = direction_ref.shape
     padded = sent_ref.shape[0] // 2
     for v, vector_ref in enumerate((direction_ref, resid_ref)):
         at = v * padded
@@ -121,6 +113,15 @@
         sent_ref[at : at + patches, :] = vector_ref[...] * factor
         if padded > patches:
             sent_ref[at + patches : at + padded, :] = jnp.zeros((padded - patches, width), F32)
+
+
+def own_kernel(
+    inverse, table_ref, ens_ref, direction_ref, resid_ref, corr_ref,
+    part_ref, scaled_ref, index_ref, sem,
+):
+    load = pltpu.make_async_copy(table_ref.at[1], index_ref, sem)
+    load.start()
+    patches = ens_ref.shape[0]
     scale(ens_ref, direction_ref.at, resid_ref.at, scaled_ref)
     load.wait()
     for start, end in blocks_of(patches):
@@ -252,9 +253,12 @@
         first_kernel, jax.ShapeDtypeStruct((GROUP, LANES), F32), [], (), [], 4000000000, 30000000
     )
     sent_shape = (2 * padded, width)
-    table = call(
+    table, sent = call(
         table_kernel,
-        jax.ShapeDtypeStruct((3, GROUP, width), F32),
+        (
+            jax.ShapeDtypeStruct((3, GROUP, width), F32),
+            jax.ShapeDtypeStruct(sent_shape, F32),
+        ),
         [],
         (first, amp_table[None], direction, resid, columns, classes),
         [VMEM] * 6,
@@ -262,12 +266,11 @@
     )
     note_above = lax.ppermute(table[0], "tile", way)
     index = [pltpu.SMEM((GROUP, width), F32), pltpu.SemaphoreType.DMA]
-    part, scaled, sent = call(
+    part, scaled = call(
         functools.partial(own_kernel, inverse),
         (
             vec,
             jax.ShapeDtypeStruct(local_shape, BF16),
-            jax.ShapeDtypeStruct(sent_shape, F32),
         ),
         index,
         (table, ens, direction, resid, corr_table),

time: 36.3 us -> 36.3 us (level)
  no operation moved by 1% of the time
where the time goes in v6:
time: 36.3 us; the launch traced here: 36.1 us
  blocking collectives  13.4 us (37%)
  starting transfers between devices  12.9 us (36%)
  Pallas kernels  8.63 us (24%)
  between operations  0.94 us (3%)
    all_to_all x1, blocking collectives, on_device(): sums = lax.all_to_all(sums, ('tile', 'mem'), 0, 0)  13.4 us
    pallas_call x7, Pallas kernels, call(): pl.pallas_call(kernel, out_shape=outs, in_specs=specs, out_specs=jax.tree...  8.63 us
    ppermute x1, starting transfers between devices, on_device(): lax.ppermute(back.astype(jnp.float16), 'tile', back_way).astype(F32)  7.31 us
    ppermute x1, starting transfers between devices, on_device(): other = lax.ppermute(mine, 'mem', [(0, 1), (1, 0)])  1.59 us
    ppermute x1, starting transfers between devices, on_device(): ens_above = lax.ppermute(ens, 'tile', way)  1.42 us
    ppermute x1, starting transfers between devices, on_device(): note_above = lax.ppermute(table[0], 'tile', way)  1.29 us
    ppermute x1, starting transfers between devices, on_device(): above = lax.ppermute(sent16, 'tile', way).astype(F32)  1.29 us
  transfers between devices with their start and end apart: 5, of which 0 were waited for; matrix products, arithmetic and copies ran while one was open for 0% of the time, Pallas kernels for 22%

profile of v6, /device:TPU:0, one launch (start us, length us, event | category | flops | bytes accessed | tf_op | source)
XLA Modules:
  0.0 36.1 jit_solution(16555735293292803767)
XLA Ops:
  0.6 0.0 copy-start.1
  0.6 0.0 copy-start.2
  0.7 0.0 copy-start.6
  0.7 0.0 copy-start.7
  0.7 0.0 copy-start.8
  0.7 0.0 copy-start
  0.7 0.0 copy-start.4
  0.7 1.4 %collective-permute-start = (bf16[150,8,256]{2,1,0:T(8,128)(2,1)}, bf16[150,8,256]{2,1,0:T(8,128)(2,1)S(1)}, u32[]{:S(2)}, u32[]{:S(2)}) collective-permute-start(bf16[150,8,256]{2,1,0:T(8,128)(2,1)} %bitcast.9), channel_id=1, source_target_pairs={{2,0},{4,2},{6,4},{8,6},{10,8},{12,10},{14,12},{16,14},{18,16},{20... | collective-permute-start | bytes 1843208 | tf_op jit(solution)/shard_map/ppermute | solution.py:251
  2.1 0.0 copy-done.1
  2.2 0.0 copy-done.2
  2.2 0.0 copy-done.6
  2.2 0.0 copy-done.7
  2.2 0.0 copy-done.8
  2.2 0.1 shard_map.105
  2.4 1.3 %collective-permute-start.2 = (f32[8,256]{1,0:T(8,128)S(1)}, f32[8,256]{1,0:T(8,128)S(1)}, u32[]{:S(2)}, u32[]{:S(2)}) collective-permute-start(f32[8,256]{1,0:T(8,128)S(1)} %slice_bitcast_fusion), channel_id=1, source_target_pairs={{2,0},{4,2},{6,4},{8,6},{10,8},{12,10},{14,12},{16,14},{18,16},{20... | collective-permute-start | bytes 24584 | tf_op jit(solution)/shard_map/ppermute | solution.py:267
  3.7 1.3 %collective-permute-start.1 = (f16[304,256]{1,0:T(8,128)(2,1)S(1)}, f16[304,256]{1,0:T(8,128)(2,1)S(1)}, u32[]{:S(2)}, u32[]{:S(2)}) collective-permute-start(f16[304,256]{1,0:T(8,128)(2,1)S(1)} %convert_element_type.12), channel_id=1, source_target_pairs={{2,0},{4,2},{6,4},{8,6},{10,8},{12,10},{14,12},{16,14},{18,16},{20... | collective-permute-start | bytes 466952 | tf_op jit(solution)/shard_map/ppermute | solution.py:281
  5.0 0.0 copy-done
  5.0 0.0 copy-done.4
  5.0 2.3 %shard_map.106 = (f32[2,150,256]{2,1,0:T(8,128)S(1)}, bf16[150,16,256]{2,1,0:T(8,128)(2,1)S(1)}) custom-call(f32[3,8,256]{2,1,0:T(8,128)S(1)} %get-tuple-element.8.table_ref, bf16[150,8,256]{2,1,0:T(8,128)(2,1)S(1)} %bitcast.10, f32[150,256]{1,0:T(8,128)S(1)} %copy-done.1, f32[150,256]{1,0:T(8,128)S(1)} %copy-done.2, bf16[9,256,256]{2,1,0:T(8,128)(2,1)S(1)} %copy-done), custom_call_target="tpu_custom_call" | custom-call | flops 943718400 | bytes 3000000 | tf_op jit(solution)/shard_map/pallas_call | solution.py:220
  7.4 1.1 %shard_map.107.products_ref = f32[3,150,16,256]{3,2,1,0:T(8,128)S(1)} custom-call(bf16[150,16,256]{2,1,0:T(8,128)(2,1)S(1)} %get-tuple-element.11.scaled_ref, bf16[9,256,256]{2,1,0:T(8,128)(2,1)S(1)} %copy-done), custom_call_target="tpu_custom_call" | custom-call | flops 943718400 | bytes 3000000 | tf_op jit(solution)/shard_map/pallas_call | solution.py:220
  8.5 0.0 copy-start.3
  8.5 0.0 collective-permute-done.2.note_above_ref
  8.5 0.0 collective-permute-done.ens_ref.ens_above_ref
  8.5 1.8 %shard_map.108.back_ref = f32[2,152,256]{2,1,0:T(8,128)S(1)} custom-call(f32[8,256]{1,0:T(8,128)S(1)} %collective-permute-done.2.note_above_ref, f32[3,8,256]{2,1,0:T(8,128)S(1)} %get-tuple-element.8.table_ref, bf16[150,8,256]{2,1,0:T(8,128)(2,1)S(1)} %collective-permute-done.ens_ref.ens_above_ref, f32[3,150,16,256]{3,2,1,0:T(8,128)S(1)} %shard_map.107.products_ref), custom_call_target="tpu_custom_call" | custom-call | flops 943718400 | bytes 3000000 | tf_op jit(solution)/shard_map/pallas_call | solution.py:220
  10.4 7.3 %collective-permute-start.3 = (f16[2,152,256]{2,1,0:T(8,128)(2,1)S(1)}, f16[2,152,256]{2,1,0:T(8,128)(2,1)S(1)}, u32[]{:S(2)}, u32[]{:S(2)}) collective-permute-start(f16[2,152,256]{2,1,0:T(8,128)(2,1)S(1)} %convert_element_type.14), channel_id=1, source_target_pairs={{0,2},{2,4},{4,6},{6,8},{8,10},{10,12},{12,14},{14,16},{16,18},{18... | collective-permute-start | bytes 466952 | tf_op jit(solution)/shard_map/ppermute | solution.py:300
  17.7 0.0 collective-permute-done.1
  17.7 0.0 copy-done.3
  17.7 2.4 %shard_map.109 = (f32[2,150,256]{2,1,0:T(8,128)S(1)}, f32[32,1,2]{2,1,0:T(1,128)S(1)}) custom-call(f32[3,8,256]{2,1,0:T(8,128)S(1)} %get-tuple-element.8.table_ref, bf16[150,8,256]{2,1,0:T(8,128)(2,1)S(1)} %collective-permute-done.ens_ref.ens_above_ref, f32[304,256]{1,0:T(8,128)S(1)} %convert_element_type.13.above_ref, ...), custom_call_target="tpu_custom_call" | custom-call | flops 943718400 | bytes 3000000 | tf_op jit(solution)/shard_map/pallas_call | solution.py:220
  20.1 0.0 copy-start.5
  20.1 0.0 collective-permute-done.3
  20.2 1.6 %collective-permute-start.4 = (f32[2,150,256]{2,1,0:T(8,128)S(1)}, f32[2,150,256]{2,1,0:T(8,128)S(1)}, u32[]{:S(2)}, u32[]{:S(2)}) collective-permute-start(f32[2,150,256]{2,1,0:T(8,128)S(1)} %fusion.mine_ref), channel_id=1, source_target_pairs={{0,1},{1,0},{2,3},{3,2},{4,5},{5,4},{6,7},{7,6},{8,9},{9,8},{10,11... | collective-permute-start | bytes 921608 | tf_op jit(solution)/shard_map/ppermute | solution.py:315
  21.8 13.4 %all_to_all.5.sums_ref = f32[32,1,2]{2,1,0:T(1,128)S(1)} all-to-all(f32[32,1,2]{2,1,0:T(1,128)S(1)} %get-tuple-element.12), channel_id=1, replica_groups=mesh['tile'=16,'mem'=2] {'tile','mem'}, dimensions={0} | all-to-all | bytes 512 | tf_op jit(solution)/shard_map/all_to_all | solution.py:319
  35.3 0.0 collective-permute-done.4.other_ref
  35.3 0.0 copy-done.5
  35.3 0.8 %shard_map.110 = (f32[150,256]{1,0:T(8,128)}, f32[150,256]{1,0:T(8,128)}) custom-call(f32[32,1,2]{2,1,0:T(1,128)S(1)} %all_to_all.5.sums_ref, f32[2,150,256]{2,1,0:T(8,128)S(1)} %fusion.mine_ref, f32[2,150,256]{2,1,0:T(8,128)S(1)} %collective-permute-done.4.other_ref, f32[150,256]{1,0:T(8,128)S(1)} %copy-done.3, f32[150,256]{1,0:T(8,128)S(1)} %copy-done.1, ...), custom_call_target="tpu_custom_call" | custom-call | flops 768000 | bytes 3000000 | tf_op jit(solution)/shard_map/pallas_call | solution.py:220
  (9 shorter events, 0.1 us)
Async XLA Ops:
  0.6 1.5 %copy-start.1 = (f32[150,256]{1,0:T(8,128)S(1)}, f32[150,256]{1,0:T(8,128)}, u32[]{:S(2)}) copy-start(f32[150,256]{1,0:T(8,128)} %direction_ref.7) | copy-start | bytes 460804
  0.6 1.5 %copy-start.2 = (f32[150,256]{1,0:T(8,128)S(1)}, f32[150,256]{1,0:T(8,128)}, u32[]{:S(2)}) copy-start(f32[150,256]{1,0:T(8,128)} %resid_ref.7) | copy-start | bytes 460804
  0.7 1.5 %copy-start.6 = (s32[150,9]{0,1:T(8,128)S(1)}, s32[150,9]{0,1:T(8,128)}, u32[]{:S(2)}) copy-start(s32[150,9]{0,1:T(8,128)} %param.16) | copy-start | bytes 16204
  0.7 1.5 %copy-start.7 = (s32[150,9]{0,1:T(8,128)S(1)}, s32[150,9]{0,1:T(8,128)}, u32[]{:S(2)}) copy-start(s32[150,9]{0,1:T(8,128)} %param.17) | copy-start | bytes 16204
  0.7 1.5 %copy-start.8 = (f32[16]{0:T(128)S(1)}, f32[16]{0:T(128)}, u32[]{:S(2)}) copy-start(f32[16]{0:T(128)} %param.15) | copy-start | bytes 196
  0.7 4.3 %copy-start = (bf16[9,256,256]{2,1,0:T(8,128)(2,1)S(1)}, bf16[9,256,256]{2,1,0:T(8,128)(2,1)}, u32[]{:S(2)}) copy-start(bf16[9,256,256]{2,1,0:T(8,128)(2,1)} %corr_ref.5) | copy-start | bytes 3538948
  0.7 4.3 %copy-start.4 = (bf16[8,150,256]{2,0,1:T(8,128)(2,1)S(1)}, bf16[8,150,256]{2,0,1:T(8,128)(2,1)}, u32[]{:S(2)}) copy-start(bf16[8,150,256]{2,0,1:T(8,128)(2,1)} %param.9) | copy-start | bytes 1843204
  0.7 7.8 %collective-permute-start = (bf16[150,8,256]{2,1,0:T(8,128)(2,1)}, bf16[150,8,256]{2,1,0:T(8,128)(2,1)S(1)}, u32[]{:S(2)}, u32[]{:S(2)}) collective-permute-start(bf16[150,8,256]{2,1,0:T(8,128)(2,1)} %bitcast.9), channel_id=1, source_target_pairs={{2,0},{4,2},{6,4},{8,6},{10,8},{12,10},{14,12},{16,14},{18,16},{20... | collective-permute-start | bytes 1843208 | tf_op jit(solution)/shard_map/ppermute | solution.py:251
  2.4 6.1 %collective-permute-start.2 = (f32[8,256]{1,0:T(8,128)S(1)}, f32[8,256]{1,0:T(8,128)S(1)}, u32[]{:S(2)}, u32[]{:S(2)}) collective-permute-start(f32[8,256]{1,0:T(8,128)S(1)} %slice_bitcast_fusion), channel_id=1, source_target_pairs={{2,0},{4,2},{6,4},{8,6},{10,8},{12,10},{14,12},{16,14},{18,16},{20... | collective-permute-start | bytes 24584 | tf_op jit(solution)/shard_map/ppermute | solution.py:267
  3.7 14.0 %collective-permute-start.1 = (f16[304,256]{1,0:T(8,128)(2,1)S(1)}, f16[304,256]{1,0:T(8,128)(2,1)S(1)}, u32[]{:S(2)}, u32[]{:S(2)}) collective-permute-start(f16[304,256]{1,0:T(8,128)(2,1)S(1)} %convert_element_type.12), channel_id=1, source_target_pairs={{2,0},{4,2},{6,4},{8,6},{10,8},{12,10},{14,12},{16,14},{18,16},{20... | collective-permute-start | bytes 466952 | tf_op jit(solution)/shard_map/ppermute | solution.py:281
  8.5 9.2 %copy-start.3 = (f32[150,256]{1,0:T(8,128)S(1)}, f32[150,256]{1,0:T(8,128)}, u32[]{:S(2)}) copy-start(f32[150,256]{1,0:T(8,128)} %clim_ref.3) | copy-start | bytes 460804
  10.4 9.8 %collective-permute-start.3 = (f16[2,152,256]{2,1,0:T(8,128)(2,1)S(1)}, f16[2,152,256]{2,1,0:T(8,128)(2,1)S(1)}, u32[]{:S(2)}, u32[]{:S(2)}) collective-permute-start(f16[2,152,256]{2,1,0:T(8,128)(2,1)S(1)} %convert_element_type.14), channel_id=1, source_target_pairs={{0,2},{2,4},{4,6},{6,8},{8,10},{10,12},{12,14},{14,16},{16,18},{18... | collective-permute-start | bytes 466952 | tf_op jit(solution)/shard_map/ppermute | solution.py:300
  20.1 15.1 %copy-start.5 = (f32[150,256]{1,0:T(8,128)S(1)}, f32[150,256]{1,0:T(8,128)}, u32[]{:S(2)}) copy-start(f32[150,256]{1,0:T(8,128)} %increment_ref.1) | copy-start | bytes 460804
  20.2 15.0 %collective-permute-start.4 = (f32[2,150,256]{2,1,0:T(8,128)S(1)}, f32[2,150,256]{2,1,0:T(8,128)S(1)}, u32[]{:S(2)}, u32[]{:S(2)}) collective-permute-start(f32[2,150,256]{2,1,0:T(8,128)S(1)} %fusion.mine_ref), channel_id=1, source_target_pairs={{0,1},{1,0},{2,3},{3,2},{4,5},{5,4},{6,7},{7,6},{8,9},{9,8},{10,11... | collective-permute-start | bytes 921608 | tf_op jit(solution)/shard_map/ppermute | solution.py:315
